TPU v7x, 128 devices: a whole 4x4x4 slice. The times are simulated.
128 devices in a mesh: pool: 128 (over x, z, y, core).
Axes of the slice: x: 4, y: 4, z: 4, core: 2. Of those that a mesh axis runs over, the one named last changes fastest.
Arguments:
- queries: bfloat16 [128, 2, 3584], P('pool'), may hold values from -120 to 120
- kv_pool: bfloat16 [4096, 256, 2, 512], P('pool'), may hold values from -6 to 6
- lengths: int32 [128], P('pool'), may hold values from 1 to 8190, 524288 in all
- block_table: int32 [4096], P('pool'), may hold values from 0 to 4095, as said below
Outputs:
- attended: bfloat16 [128, 2, 3584], P('pool')
Inputs may be any that keep to these rules, and one draw needn't show every extreme that they name: `block_table`: a permutation of the pool blocks; with the requests numbered in groups of 1 per owner index o and G groups, the entry at place j of the 32 entries of group o is a block numbered from ((o + s_j) mod G) * 32 to that + 31, where s_j = (j * G) // 32, except s_0 = 1 when G > 32. The pool holds positions 0 to lengths + 1 of each request.
All inputs are finite; a program needn't handle non-finite values. No bound on the sum of `lengths` on one device may be relied on, other than what follows from the above.
Results may differ from a plain program's by a relative error of at most 0.0095.
Values may be sent and summed in bfloat16 or wider, within the bound.
No kernel may reach another device: no remote copies, remote signals or barrier semaphores. Data moves between devices by JAX's collectives and lax.ppermute only.
A program may use at most 192 MiB of HBM per device.

v0:
```python
import jax
import jax.numpy as jnp
from jax import lax
from jax.sharding import PartitionSpec as P

KVH = 4
GROUP = 7
HEAD = 128
BLOCK = 256


def body(queries, kv_pool, lengths, block_table):
    every_query, every_length, every_entry = (
        lax.all_gather(queries, "pool", axis=0, tiled=True),
        lax.all_gather(lengths, "pool", axis=0, tiled=True),
        lax.all_gather(block_table, "pool", axis=0, tiled=True),
    )
    slot_count = kv_pool.shape[0]
    request_count = every_query.shape[0]
    table_width = every_entry.shape[0] // request_count
    score_scale = 1.0 / HEAD**0.5
    slot_ids = lax.axis_index("pool") * slot_count + jnp.arange(slot_count, dtype=jnp.int32)
    matches = every_entry[None, :] == slot_ids[:, None]
    entry_index = jnp.sum(
        jnp.where(matches, jnp.arange(every_entry.shape[0], dtype=jnp.int32)[None, :], 0), axis=1
    )
    owner_row = entry_index // table_width
    block_pos = entry_index % table_width
    held_query = every_query[owner_row].reshape(slot_count, 2, KVH, GROUP, HEAD)
    slot_keys = kv_pool[:, :, 0, :].reshape(slot_count, BLOCK, KVH, HEAD)
    slot_values = kv_pool[:, :, 1, :].reshape(slot_count, BLOCK, KVH, HEAD)
    scores = (
        jnp.einsum("stkgd,spkd->stkgp", held_query, slot_keys, preferred_element_type=jnp.float32)
        * score_scale
    )
    positions = block_pos[:, None] * BLOCK + jnp.arange(BLOCK, dtype=jnp.int32)[None, :]
    visible_end = every_length[owner_row][:, None] + 1 + jnp.arange(2, dtype=jnp.int32)[None, :]
    visible = positions[:, None, :] < visible_end[:, :, None]
    scores = jnp.where(visible[:, :, None, None, :], scores, -jnp.inf)
    slot_max = jnp.max(scores, axis=-1)
    member = owner_row[None, :] == jnp.arange(request_count, dtype=jnp.int32)[:, None]
    request_max = jnp.max(
        jnp.where(member[:, :, None, None, None], slot_max[None], -jnp.inf), axis=1
    )
    member_weight = member.astype(jnp.float32)
    row_peak = lax.pmax(request_max, "pool")
    unscaled = jnp.exp(scores - row_peak[owner_row][..., None])
    denominator = jnp.sum(unscaled, axis=-1)
    weights = unscaled.astype(jnp.bfloat16)
    numerator = jnp.einsum(
        "stkgp,spkd->stkgd", weights, slot_values, preferred_element_type=jnp.float32
    )
    numerator, denominator = (numerator, denominator)
    request_numer = jnp.einsum(
        "rs,stkgd->rtkgd", member_weight, numerator, precision=lax.Precision.HIGHEST
    )
    request_total = jnp.einsum(
        "rs,stkg->rtkg", member_weight, denominator, precision=lax.Precision.HIGHEST
    )
    request_numer, request_total = (request_numer, request_total)
    own_numer, own_total = (
        lax.psum_scatter(request_numer, "pool", scatter_dimension=0, tiled=True),
        lax.psum_scatter(request_total, "pool", scatter_dimension=0, tiled=True),
    )
    attended = own_numer / own_total[..., None]
    return attended.reshape(own_numer.shape[0], 2, KVH * GROUP * HEAD).astype(jnp.bfloat16)


def solution(mesh):
    placed = (P("pool", None, None), P("pool", None, None, None), P("pool"), P("pool"))
    return jax.shard_map(
        body, mesh=mesh, in_specs=placed, out_specs=P("pool", None, None), check_vma=False
    )
```

profile of v0, /device:TPU:0, one launch (start us, length us, event | category | flops | bytes accessed | tf_op | source)
XLA Modules:
  0.0 429.8 jit_solution(5202961204684764070)
XLA Ops:
  6.5 0.0 all-gather.2.cloned.1.call-start
  6.5 0.7 all-gather.2.cloned.1.call-update
  7.3 0.0 all-reduce.7.cloned.1.call-start
  7.3 32.8 %fusion.22 = (bf16[32,256,1,512]{3,2,1,0:T(2,128)(2,1)}, bf16[32,256,1,512]{3,2,1,0:T(2,128)(2,1)}) fusion(bf16[32,256,2,512]{3,2,1,0:T(2,128)(2,1)} %param.5), kind=kLoop, calls=%fused_computation.51 | loop fusion | bytes 33554432 | tf_op jit(solution)/shard_map/slice | solution.py:30
  40.1 35.5 %copy.55 = bf16[32,256,1,512]{1,3,0,2:T(8,128)(2,1)} copy(bf16[32,256,1,512]{3,2,1,0:T(2,128)(2,1)} %get-tuple-element.8) | data formatting | bytes 16777216
  76.3 0.0 copy-start
  76.3 35.4 %copy.54 = bf16[32,256,1,512]{1,3,0,2:T(8,128)(2,1)} copy(bf16[32,256,1,512]{3,2,1,0:T(2,128)(2,1)} %get-tuple-element.7) | data formatting | bytes 16777216
  111.7 0.1 dynamic-update-slice.1
  111.8 0.0 copy-done
  111.8 0.3 dynamic-update-slice
  112.1 68.4 %all-reduce.4 = (s32[4096]{0:T(1024)S(1)}, s32[128]{0:T(128)S(1)}) all-reduce(s32[4096]{0:T(1024)S(1)} %dynamic-update-slice, s32[128]{0:T(128)S(1)} %dynamic-update-slice.1), channel_id=1, replica_groups=mesh['pool'=128] {'pool'}, use_global_device_ids=true, to_apply=%add | all-reduce | flops 4224 | bytes 33792
  180.5 0.2 select_reduce_fusion.1
  180.8 0.7 gather_fusion
  181.5 0.1 iota_compare_fusion
  181.6 0.1 iota_add_fusion.1
  181.6 0.1 iota_add_fusion
  181.7 0.1 broadcast_compare_fusion
  181.8 0.0 all-gather.2.cloned.1.call-done
  181.9 3.0 gather_fusion.1
  184.9 0.4 reshape.211
  185.2 4.9 %bitcast_reduce_fusion = (f32[32,2,4,7]{3,1,2,0:T(2,128)S(1)}, f32[32,4,2,7,256]{4,3,2,1,0:T(8,128)S(1)}) fusion(pred[32,2,256]{2,1,0:T(4,128)(4,1)S(1)} %broadcast_compare_fusion, bf16[32,256,4,128,1]{1,3,4,2,0:T(8,128)(2,1)} %bitcast.48, bf16[32,2,4,7,128]{4,3,2,1,0:T(8,128)(2,1)S(1)} %reshape.211), kind=kOutput, calls=%fused_computation.4 | convolution fusion | flops 118814976 | bytes 10705920 | tf_op jit(solution)/shard_map/stkgd,spkd->stkgp/dot_general | solution.py:33
  190.2 0.1 copy.33
  190.3 0.3 select_reduce_fusion
  190.6 0.3 copy.34
  190.9 65.4 %pmax.7 = f32[128,2,4,7]{3,2,1,0:T(4,128)S(1)} all-reduce(f32[128,2,4,7]{3,2,1,0:T(4,128)S(1)} %copy.34), channel_id=1, replica_groups=mesh['pool'=128] {'pool'}, use_global_device_ids=true, to_apply=%region_3.4 | all-reduce | flops 7168 | bytes 57344 | tf_op jit(solution)/shard_map/pmax | solution.py:46
  256.4 0.6 gather_fusion.2
  257.0 0.1 copy.35
  257.1 5.7 %convolution_bitcast_fusion = f32[32,2,4,7,128]{4,3,1,2,0:T(8,128)S(1)} fusion(bf16[32,256,4,128,1]{1,3,4,2,0:T(8,128)(2,1)} %bitcast.49, f32[32,4,2,7,256]{4,3,2,1,0:T(8,128)S(1)} %get-tuple-element.12, f32[32,2,4,7]{3,1,2,0:T(2,128)S(1)} %copy.35, pred[32,2,256]{2,1,0:T(4,128)(4,1)S(1)} %broadcast_compare_fusion), kind=kOutput, calls=%fused_computation.9 | convolution fusion | flops 119275520 | bytes 11164672 | tf_op jit(solution)/shard_map/stkgp,spkd->stkgd/dot_general | solution.py:50
  262.8 2.0 fusion.8
  264.8 4.2 copy.39
  269.0 0.0 all-reduce.7.cloned.1.call-update
  269.0 1.2 fusion.1
  270.2 0.5 fusion.12
  270.7 0.3 copy.41
  271.1 68.5 %all-reduce.3 = f32[128,2,4,7]{3,2,1,0:T(4,128)S(1)} all-reduce(f32[128,2,4,7]{3,2,1,0:T(4,128)S(1)} %copy.41), channel_id=3, replica_groups=mesh['pool'=128] {'pool'}, use_global_device_ids=true, to_apply=%region_6.7.clone | all-reduce | flops 7168 | bytes 57344
  339.6 0.1 copy.42
  339.7 81.8 %all-reduce.7.cloned.1.call-done = f32[128,2,4,7,128]{4,2,3,1,0:T(4,128)} async-done(((f32[128,2,4,7,128]{4,2,3,1,0:T(4,128)}), f32[128,2,4,7,128]{4,2,3,1,0:T(4,128)}) %all-reduce.7.cloned.1.call-update) | async-done | bytes 3670032
  421.5 0.8 fusion.14
  422.4 0.6 convert_element_type.20
  (9 shorter events, 0.1 us)
Async XLA Ops:
  6.5 175.3 %all-gather.2.cloned.1.call-start = ((), (), s32[]{:S(2)}) async-start(), calls=%async_computation | async-start | bytes 1849344 | tf_op jit(solution)/shard_map/all_gather | solution.py:14
  7.3 414.3 %all-reduce.7.cloned.1.call-start = ((), (), s32[]{:S(2)}) async-start(), calls=%async_computation.1 | async-start | bytes 7340032
  76.3 35.5 %copy-start = (s32[32]{0:T(128)S(1)}, s32[32]{0:T(128)}, u32[]{:S(2)}) copy-start(s32[32]{0:T(128)} %param.7) | copy-start | bytes 388
Sparse Core Ops, SparseCore 0:
  10.3 67.4 all-gather.1
  269.2 152.3 all-reduce.6
where the time goes:
time: 433 us; the launch traced here: 430 us
  blocking collectives  202 us (47%)
  local copies, waits for them, and re-layouts  115 us (27%)
  waiting for transfers between devices  82.6 us (19%)
  between operations  14.2 us (3%)
  matrix products  13.1 us (3%)
    unnamed x2, blocking collectives  137 us
    unnamed x3, waiting for transfers between devices  82.6 us
    unnamed x8, local copies, waits for them, and re-layouts  71.3 us
    pmax x1, blocking collectives, body(): row_peak = lax.pmax(request_max, 'pool')  65.4 us
    slice x1, local copies, waits for them, and re-layouts, body(): slot_keys = kv_pool[:, :, 0, :].reshape(slot_count, BLOCK, KVH, HEAD)  32.8 us
  transfers between devices with their start and end apart: 2, of which 1 were waited for; matrix products, arithmetic and copies ran while one was open for 25% of the time, Pallas kernels for 0%

commit v1 on v0

v1 whole, which is shorter than its diff:
```python
import jax
import jax.numpy as jnp
from jax import lax
from jax.experimental import pallas as pl
from jax.experimental.pallas import tpu as pltpu
from jax.sharding import PartitionSpec as P

KVH = 4
GROUP = 7
HEAD = 128
BLOCK = 256
PLACES = 32
DEVICES = 128
STRIDE = DEVICES // PLACES
ROWS = 2 * GROUP
PAD = 16
QROWS = KVH * ROWS
PROWS = KVH * PAD
CHUNK = PROWS + PAD
LINES = BLOCK * KVH * 2
TILE = 256
META = ROWS
UNROLL = 2
LOG2_SCALE = 1.4426950408889634 / HEAD**0.5
HIDDEN = -(2.0**120)
GROUPS = [[STRIDE * i + r for i in range(PLACES)] for r in range(STRIDE)]
NEXT = [(d, (d + 1) % DEVICES) for d in range(DEVICES)]
PREVIOUS = [((d + 1) % DEVICES, d) for d in range(DEVICES)]


def my_member():
    return lax.axis_index("pool") // STRIDE


def iota(shape, dim):
    return lax.broadcasted_iota(jnp.int32, shape, dim)


def pad_matrix(shape, padded_dim):
    padded, plain = iota(shape, padded_dim), iota(shape, 1 - padded_dim)
    hit = (padded % PAD < ROWS) & (padded // PAD * ROWS + padded % PAD == plain)
    return jnp.where(hit, 1.0, 0.0).astype(jnp.bfloat16)


def split3(x):
    hi = x.astype(jnp.bfloat16).astype(jnp.float32)
    rest = x - hi
    mid = rest.astype(jnp.bfloat16).astype(jnp.float32)
    return hi, mid, rest - mid


def pack_kernel(length_ref, table_ref, query_ref, sent_ref, first_ref):
    member = my_member()
    padded = jnp.dot(
        pad_matrix((PROWS, QROWS), 0), query_ref[...], preferred_element_type=jnp.float32
    )
    length = length_ref[0]
    row, lane = iota((PAD, HEAD), 0), iota((PAD, HEAD), 1)
    is_meta = row == META
    length_lanes = jnp.where(lane == 1, length // 128, jnp.where(lane == 2, length % 128, 0))
    head = padded[:PAD]
    rest = padded[PAD:].astype(jnp.bfloat16)

    def chunk_head(place):
        slot = table_ref[place] % PLACES
        meta = jnp.where(lane == 0, slot, length_lanes).astype(jnp.float32)
        return jnp.where(is_meta, meta, head).astype(jnp.bfloat16)

    for i in range(PLACES):
        sent_ref[i, :PAD, :] = chunk_head(lax.rem(i + PLACES - member, PLACES))
        sent_ref[i, PAD:, :] = rest
    first_ref[:PAD, :] = chunk_head(0)
    first_ref[PAD:, :] = rest


def attend_kernel(
    held_ref, first_ref, lines_ref, out_ref, out_first_ref, meta_vmem, meta_smem, todo, meta_sem
):
    member = my_member()
    meta = jnp.where(
        iota((PLACES, PAD, HEAD), 1) == META, held_ref[:, :PAD, :].astype(jnp.float32), 0.0
    )
    meta = jnp.sum(meta, axis=1)
    meta_first = jnp.sum(
        jnp.where(iota((PAD, HEAD), 0) == META, first_ref[:PAD, :].astype(jnp.float32), 0.0),
        axis=0,
        keepdims=True,
    )
    meta = jnp.where(iota((PLACES, HEAD), 0) == member, meta_first, meta)
    meta_vmem[...] = meta.astype(jnp.int32)
    copy = pltpu.make_async_copy(meta_vmem, meta_smem, meta_sem)
    copy.start()

    lane = iota((PAD, HEAD), 1)
    head_of_lane = lane % 8 // 2
    token = iota((PAD, HEAD), 0) % 2
    value_of = [
        jnp.where(lane % 8 == 2 * k + 1, 1.0, 0.0).astype(jnp.bfloat16) for k in range(KVH)
    ]

    def meta_rows(peak, total):
        parts = (*split3(peak), *split3(total))
        rows = jnp.zeros_like(peak)
        for g, part in enumerate(parts):
            rows = jnp.where(lane // 8 == g, part, rows)
        return rows.astype(jnp.bfloat16)

    no_numer = jnp.zeros((PROWS, HEAD), jnp.bfloat16)
    no_meta = meta_rows(jnp.full((PAD, HEAD), HIDDEN), jnp.zeros((PAD, HEAD)))
    for i in range(PLACES):
        out_ref[i, :PROWS, :] = no_numer
        out_ref[i, PROWS:, :] = no_meta
    copy.wait()

    def place_of(i):
        return lax.rem(member + PLACES - i, PLACES)

    def length_of(i):
        return meta_smem[i, 1] * 128 + meta_smem[i, 2]

    def note(i, count):
        seen = place_of(i) * BLOCK < length_of(i) + 2

        @pl.when(seen)
        def _():
            todo[count] = i

        return count + seen.astype(jnp.int32)

    count = lax.fori_loop(0, PLACES, note, jnp.int32(0))

    def attend(i):
        slot = meta_smem[i, 0]
        query = jnp.where(i == member, first_ref[...], held_ref[i])
        limit = 8 * (length_of(i) + 1 - place_of(i) * BLOCK + token)
        scores = []
        for n in range(LINES // TILE):
            tile = lines_ref[slot, n * TILE : (n + 1) * TILE, :]
            every = lax.dot_general(
                query, tile, (((1,), (1,)), ((), ())), preferred_element_type=jnp.float32
            )
            for half in range(TILE // HEAD):
                part = every[:, half * HEAD : (half + 1) * HEAD]
                own = part[(KVH - 1) * PAD :]
                for k in range(KVH - 1):
                    own = jnp.where(head_of_lane == k, part[k * PAD : (k + 1) * PAD], own)
                at = n * TILE + half * HEAD
                scores.append(jnp.where(lane < limit - at, own, HIDDEN))
        peak = scores[0]
        for part in scores[1:]:
            peak = jnp.maximum(peak, part)
        for shift in (8, 16, 32, 64):
            peak = jnp.maximum(peak, pltpu.roll(peak, shift, 1))
        total = jnp.zeros((PAD, HEAD), jnp.float32)
        numer = jnp.zeros((PROWS, HEAD), jnp.float32)
        for n in range(LINES // TILE):
            tile = lines_ref[slot, n * TILE : (n + 1) * TILE, :]
            halves = []
            for half in range(TILE // HEAD):
                unscaled = jnp.exp2((scores[n * (TILE // HEAD) + half] - peak) * LOG2_SCALE)
                total = total + unscaled
                moved = pltpu.roll(unscaled, 1, 1).astype(jnp.bfloat16)
                halves.append(jnp.concatenate([moved * value_of[k] for k in range(KVH)], axis=0))
            weights = jnp.concatenate(halves, axis=1)
            numer = numer + jnp.dot(weights, tile, preferred_element_type=jnp.float32)
        for shift in (8, 16, 32, 64):
            total = total + pltpu.roll(total, shift, 1)
        out_ref[i, :PROWS, :] = numer.astype(jnp.bfloat16)
        out_ref[i, PROWS:, :] = meta_rows(peak, total)

    def step(s, carry):
        for u in range(UNROLL):
            attend(todo[jnp.minimum(s * UNROLL + u, count - 1)])
        return carry

    lax.fori_loop(0, (count + UNROLL - 1) // UNROLL, step, 0)
    out_first_ref[...] = out_ref[member]
    out_ref[member, :PROWS, :] = no_numer
    out_ref[member, PROWS:, :] = no_meta


def merge_kernel(part_ref, first_ref, out_ref):
    at, lane = iota((HEAD, HEAD), 0), iota((HEAD, HEAD), 1)
    meta = part_ref[:, PROWS:, :].reshape(PLACES * PAD, HEAD)
    meta_first = first_ref[PROWS:, :]
    merged = []
    for k in range(KVH):
        peak_of = ((at % 8 == 2 * k) & (at < 24)).astype(jnp.float32).astype(jnp.bfloat16)
        total_of = ((at % 8 == 2 * k) & (at >= 24) & (at < 48)).astype(jnp.float32).astype(jnp.bfloat16)

        def spread(rows, of):
            return jnp.dot(rows, of, preferred_element_type=jnp.float32)

        peak = spread(meta, peak_of).reshape(PLACES, PAD, HEAD)
        total = spread(meta, total_of).reshape(PLACES, PAD, HEAD)
        peak_first, total_first = spread(meta_first, peak_of), spread(meta_first, total_of)
        top = jnp.maximum(jnp.max(peak, axis=0), peak_first)
        share = jnp.exp2((peak - top[None]) * LOG2_SCALE)
        share_first = jnp.exp2((peak_first - top) * LOG2_SCALE)
        rows = slice(k * PAD, (k + 1) * PAD)
        numer = part_ref[:, rows, :].astype(jnp.float32)
        numer = jnp.sum(share * numer, axis=0) + share_first * first_ref[rows, :].astype(jnp.float32)
        denom = jnp.sum(share * total, axis=0) + share_first * total_first
        merged.append((numer / denom).astype(jnp.bfloat16))
    merged = jnp.concatenate(merged, axis=0)
    out_ref[...] = jnp.dot(
        pad_matrix((QROWS, PROWS), 1), merged, preferred_element_type=jnp.float32
    ).astype(jnp.bfloat16)


def vmem(count):
    return [pl.BlockSpec(memory_space=pltpu.VMEM)] * count


def smem(count):
    return [pl.BlockSpec(memory_space=pltpu.SMEM)] * count


def bf16(*shape):
    return jax.ShapeDtypeStruct(shape, jnp.bfloat16)


def pack(lengths, table, query):
    return pl.pallas_call(
        pack_kernel,
        in_specs=smem(2) + vmem(1),
        out_specs=vmem(2),
        out_shape=[bf16(PLACES, PROWS, HEAD), bf16(PROWS, HEAD)],
    )(lengths, table, query)


def attend_blocks(held, first, lines):
    return pl.pallas_call(
        attend_kernel,
        in_specs=vmem(3),
        out_specs=vmem(2),
        out_shape=[bf16(PLACES, CHUNK, HEAD), bf16(CHUNK, HEAD)],
        scratch_shapes=[
            pltpu.VMEM((PLACES, HEAD), jnp.int32),
            pltpu.SMEM((PLACES, HEAD), jnp.int32),
            pltpu.SMEM((PLACES,), jnp.int32),
            pltpu.SemaphoreType.DMA,
        ],
        compiler_params=pltpu.CompilerParams(vmem_limit_bytes=16 * 2**20),
    )(held, first, lines)


def merge(parts, first):
    return pl.pallas_call(
        merge_kernel,
        in_specs=vmem(2),
        out_specs=vmem(1)[0],
        out_shape=bf16(QROWS, HEAD),
    )(parts, first)


def body(queries, kv_pool, lengths, block_table):
    query = (
        queries.reshape(1, 2, KVH * GROUP, HEAD).transpose(0, 2, 1, 3).reshape(QROWS, HEAD)
    )
    lines = (
        kv_pool.reshape(PLACES, BLOCK, 2, KVH, HEAD)
        .transpose(0, 1, 3, 2, 4)
        .reshape(PLACES, LINES, HEAD)
    )
    lines = pltpu.with_memory_space_constraint(lines, pltpu.VMEM)
    sent, first = pack(lengths, block_table, query)
    first = lax.ppermute(first, "pool", NEXT)
    held = lax.all_to_all(sent, "pool", 0, 0, tiled=True, axis_index_groups=GROUPS)
    parts, part_first = attend_blocks(held, first, lines)
    part_first = lax.ppermute(part_first, "pool", PREVIOUS)
    parts = lax.all_to_all(parts, "pool", 0, 0, tiled=True, axis_index_groups=GROUPS)
    merged = merge(parts, part_first)
    return (
        merged.reshape(1, KVH * GROUP, 2, HEAD)
        .transpose(0, 2, 1, 3)
        .reshape(1, 2, KVH * GROUP * HEAD)
    )


def solution(mesh):
    placed = (P("pool", None, None), P("pool", None, None, None), P("pool"), P("pool"))
    return jax.shard_map(
        body, mesh=mesh, in_specs=placed, out_specs=P("pool", None, None), check_vma=False
    )
```

time: 433 us -> 76 us (0.18)
  blocking collectives: 202 us -> 0 us
  local copies, waits for them, and re-layouts: 115 us -> 9.3 us
  waiting for transfers between devices: 82.6 us -> 24.6 us
  Pallas kernels: 0 us -> 21.4 us
  starting transfers between devices: 0.04 us -> 19.7 us
  between operations: 14.2 us -> 0.69 us
  matrix products: 13.1 us -> 0 us
    unnamed x2 -> x0, blocking collectives: 137 us -> none
    unnamed x3 -> x0, waiting for transfers between devices: 82.6 us -> none
    pmax x1 -> x0, blocking collectives: 65.4 us -> none  [body(): row_peak = lax.pmax(request_max, 'pool')]
    unnamed x8 -> x6, local copies, waits for them, and re-layouts: 71.3 us -> 6.62 us
    slice x1 -> x0, local copies, waits for them, and re-layouts: 32.8 us -> none  [body(): slot_keys = kv_pool[:, :, 0, :].reshape(slot_count, BLOCK, KVH, HEAD)]
    pallas_call x0 -> x3, Pallas kernels: none -> 21.4 us  [the longest x1 17.3 us: attend_blocks(): pl.pallas_call(attend_kernel, in_specs=vmem(3), out_specs=vmem(2), out_sh...]
    all_to_all x0 -> x2, starting transfers between devices: none -> 16.2 us  [the longest x1 10.9 us: body(): lax.all_to_all(sent, 'pool', 0, 0, tiled=True, axis_index_groups=GROUPS)]
    ppermute x0 -> x2, waiting for transfers between devices: none -> 14.1 us  [the longest x1 12 us: body(): first = lax.ppermute(first, 'pool', NEXT)]
  transfers between devices with their start and end apart: 2 -> 4, of which waited for: 1 -> 4; matrix products, arithmetic and copies ran while one was open for 25% -> 0% of each run, Pallas kernels for 0% -> 0%
where the time goes in v1:
time: 76 us; the launch traced here: 75.6 us
  waiting for transfers between devices  24.6 us (32%)
  Pallas kernels  21.4 us (28%)
  starting transfers between devices  19.7 us (26%)
  local copies, waits for them, and re-layouts  9.3 us (12%)
    pallas_call x1, Pallas kernels, attend_blocks(): pl.pallas_call(attend_kernel, in_specs=vmem(3), out_specs=vmem(2), out_sh...  17.3 us
    ppermute x1, waiting for transfers between devices, body(): first = lax.ppermute(first, 'pool', NEXT)  12 us
    all_to_all x1, starting transfers between devices, body(): lax.all_to_all(sent, 'pool', 0, 0, tiled=True, axis_index_groups=GROUPS)  10.9 us
    all_to_all x1, waiting for transfers between devices, body(): lax.all_to_all(parts, 'pool', 0, 0, tiled=True, axis_index_groups=GROUPS)  9.07 us
    unnamed x6, local copies, waits for them, and re-layouts  6.62 us
    all_to_all x1, starting transfers between devices, body(): lax.all_to_all(parts, 'pool', 0, 0, tiled=True, axis_index_groups=GROUPS)  5.32 us
    ppermute x1, starting transfers between devices, body(): part_first = lax.ppermute(part_first, 'pool', PREVIOUS)  3.4 us
    pallas_call x1, Pallas kernels, merge(): pl.pallas_call(merge_kernel, in_specs=vmem(2), out_specs=vmem(1)[0], out_...  2.39 us
  transfers between devices with their start and end apart: 4, of which 4 were waited for; matrix products, arithmetic and copies ran while one was open for 0% of the time, Pallas kernels for 0%

profile of v1, /device:TPU:0, one launch (start us, length us, event | category | flops | bytes accessed | tf_op | source)
XLA Modules:
  0.0 75.6 jit_solution(6802243046275129908)
XLA Ops:
  0.7 0.7 reshape.18
  1.4 0.6 copy.8
  2.0 1.7 %shard_map.46 = (bf16[32,64,128]{2,1,0:T(8,128)(2,1)}, bf16[64,128]{1,0:T(8,128)(2,1)}) custom-call(s32[1]{0:T(128)S(6)} %copy.13.length_ref, s32[32]{0:T(128)} %table_ref.1, bf16[56,128]{1,0:T(8,128)(2,1)} %bitcast.14), custom_call_target="tpu_custom_call" | custom-call | tf_op jit(solution)/shard_map/pallas_call | solution.py:224
  3.7 10.9 %all-to-all-start = ((bf16[32,64,128]{2,1,0:T(8,128)(2,1)}), bf16[32,64,128]{2,1,0:T(8,128)(2,1)S(1)}, u32[]{:S(2)}, u32[]{:S(2)}) async-start(bf16[32,64,128]{2,1,0:T(8,128)(2,1)} %get-tuple-element.9), calls=%async_computation | async-start | bytes 1048576 | tf_op jit(solution)/shard_map/all_to_all | solution.py:269
  14.6 0.1 collective-permute-start
  14.7 12.0 %collective-permute-done.first_ref = bf16[64,128]{1,0:T(8,128)(2,1)S(1)} collective-permute-done((bf16[64,128]{1,0:T(8,128)(2,1)}, bf16[64,128]{1,0:T(8,128)(2,1)S(1)}, u32[]{:S(2)}, u32[]{:S(2)}) %collective-permute-start) | collective-permute-done | bytes 16416 | tf_op jit(solution)/shard_map/ppermute | solution.py:268
  26.7 1.4 %all-to-all-done.held_ref = bf16[32,64,128]{2,1,0:T(8,128)(2,1)S(1)} async-done(((bf16[32,64,128]{2,1,0:T(8,128)(2,1)}), bf16[32,64,128]{2,1,0:T(8,128)(2,1)S(1)}, u32[]{:S(2)}, u32[]{:S(2)}) %all-to-all-start) | async-done | bytes 524320 | tf_op jit(solution)/shard_map/all_to_all | solution.py:269
  28.1 0.0 copy-start
  28.1 5.8 %copy-done = bf16[32,256,2,512]{3,2,1,0:T(2,128)(2,1)S(1)} copy-done((bf16[32,256,2,512]{3,2,1,0:T(2,128)(2,1)S(1)}, bf16[32,256,2,512]{3,2,1,0:T(2,128)(2,1)}, u32[]{:S(2)}) %copy-start) | copy-done | bytes 16777240
  33.9 17.3 %shard_map.47 = (bf16[32,80,128]{2,1,0:T(8,128)(2,1)}, bf16[80,128]{1,0:T(8,128)(2,1)S(1)}) custom-call(bf16[32,64,128]{2,1,0:T(8,128)(2,1)S(1)} %all-to-all-done.held_ref, bf16[64,128]{1,0:T(8,128)(2,1)S(1)} %collective-permute-done.first_ref, bf16[32,2048,128]{2,1,0:T(8,128)(2,1)S(1)} %bitcast.11), custom_call_target="tpu_custom_call" | custom-call | tf_op jit(solution)/shard_map/pallas_call | solution.py:233
  51.2 5.3 %all-to-all-start.1 = ((bf16[32,80,128]{2,1,0:T(8,128)(2,1)}), bf16[32,80,128]{2,1,0:T(8,128)(2,1)S(1)}, u32[]{:S(2)}, u32[]{:S(2)}) async-start(bf16[32,80,128]{2,1,0:T(8,128)(2,1)} %get-tuple-element.11), calls=%async_computation.1 | async-start | bytes 1310720 | tf_op jit(solution)/shard_map/all_to_all | solution.py:272
  56.5 3.4 %collective-permute-start.1 = (bf16[80,128]{1,0:T(8,128)(2,1)S(1)}, bf16[80,128]{1,0:T(8,128)(2,1)S(1)}, u32[]{:S(2)}, u32[]{:S(2)}) collective-permute-start(bf16[80,128]{1,0:T(8,128)(2,1)S(1)} %get-tuple-element.12), channel_id=1, source_target_pairs={{1,0},{2,1},{3,2},{4,3},{5,4},{6,5},{7,6},{8,7},{9,8},{10,9},{11,1... | collective-permute-start | bytes 61448 | tf_op jit(solution)/shard_map/ppermute | solution.py:271
  59.9 2.0 %collective-permute-done.1.first_ref = bf16[80,128]{1,0:T(8,128)(2,1)S(1)} collective-permute-done((bf16[80,128]{1,0:T(8,128)(2,1)S(1)}, bf16[80,128]{1,0:T(8,128)(2,1)S(1)}, u32[]{:S(2)}, u32[]{:S(2)}) %collective-permute-start.1) | collective-permute-done | bytes 20512 | tf_op jit(solution)/shard_map/ppermute | solution.py:271
  62.0 0.0 copy-start.2
  62.0 9.1 %all-to-all-done.1.part_ref = bf16[32,80,128]{2,1,0:T(8,128)(2,1)S(1)} async-done(((bf16[32,80,128]{2,1,0:T(8,128)(2,1)}), bf16[32,80,128]{2,1,0:T(8,128)(2,1)S(1)}, u32[]{:S(2)}, u32[]{:S(2)}) %all-to-all-start.1) | async-done | bytes 655392 | tf_op jit(solution)/shard_map/all_to_all | solution.py:272
  71.1 0.0 copy-done.2
  71.1 0.0 copy-start.1
  71.1 0.8 %copy-done.1 = bf16[32,80,128]{2,1,0:T(8,128)(2,1)} copy-done((bf16[32,80,128]{2,1,0:T(8,128)(2,1)}, bf16[32,80,128]{2,1,0:T(8,128)(2,1)S(1)}, u32[]{:S(2)}) %copy-start.1) | copy-done | bytes 655384
  71.9 2.4 %shard_map.48 = bf16[56,128]{1,0:T(8,128)(2,1)} custom-call(bf16[32,80,128]{2,1,0:T(8,128)(2,1)} %copy-done.1, bf16[80,128]{1,0:T(8,128)(2,1)} %copy-done.2), custom_call_target="tpu_custom_call" | custom-call | tf_op jit(solution)/shard_map/pallas_call | solution.py:249
  74.3 0.7 copy.12
  75.0 0.6 reshape.23
Async XLA Ops:
  3.7 24.4 %all-to-all-start = ((bf16[32,64,128]{2,1,0:T(8,128)(2,1)}), bf16[32,64,128]{2,1,0:T(8,128)(2,1)S(1)}, u32[]{:S(2)}, u32[]{:S(2)}) async-start(bf16[32,64,128]{2,1,0:T(8,128)(2,1)} %get-tuple-element.9), calls=%async_computation | async-start | bytes 1048576 | tf_op jit(solution)/shard_map/all_to_all | solution.py:269
  14.6 12.1 %collective-permute-start = (bf16[64,128]{1,0:T(8,128)(2,1)}, bf16[64,128]{1,0:T(8,128)(2,1)S(1)}, u32[]{:S(2)}, u32[]{:S(2)}) collective-permute-start(bf16[64,128]{1,0:T(8,128)(2,1)} %get-tuple-element.10), channel_id=1, source_target_pairs={{0,1},{1,2},{2,3},{3,4},{4,5},{5,6},{6,7},{7,8},{8,9},{9,10},{10,1... | collective-permute-start | bytes 49160 | tf_op jit(solution)/shard_map/ppermute | solution.py:268
  28.1 5.8 %copy-start = (bf16[32,256,2,512]{3,2,1,0:T(2,128)(2,1)S(1)}, bf16[32,256,2,512]{3,2,1,0:T(2,128)(2,1)}, u32[]{:S(2)}) copy-start(bf16[32,256,2,512]{3,2,1,0:T(2,128)(2,1)} %param.5) | copy-start | bytes 50331652
  51.2 19.8 %all-to-all-start.1 = ((bf16[32,80,128]{2,1,0:T(8,128)(2,1)}), bf16[32,80,128]{2,1,0:T(8,128)(2,1)S(1)}, u32[]{:S(2)}, u32[]{:S(2)}) async-start(bf16[32,80,128]{2,1,0:T(8,128)(2,1)} %get-tuple-element.11), calls=%async_computation.1 | async-start | bytes 1310720 | tf_op jit(solution)/shard_map/all_to_all | solution.py:272
  56.5 5.4 %collective-permute-start.1 = (bf16[80,128]{1,0:T(8,128)(2,1)S(1)}, bf16[80,128]{1,0:T(8,128)(2,1)S(1)}, u32[]{:S(2)}, u32[]{:S(2)}) collective-permute-start(bf16[80,128]{1,0:T(8,128)(2,1)S(1)} %get-tuple-element.12), channel_id=1, source_target_pairs={{1,0},{2,1},{3,2},{4,3},{5,4},{6,5},{7,6},{8,7},{9,8},{10,9},{11,1... | collective-permute-start | bytes 61448 | tf_op jit(solution)/shard_map/ppermute | solution.py:271
  62.0 9.1 %copy-start.2 = (bf16[80,128]{1,0:T(8,128)(2,1)}, bf16[80,128]{1,0:T(8,128)(2,1)S(1)}, u32[]{:S(2)}) copy-start(bf16[80,128]{1,0:T(8,128)(2,1)S(1)} %collective-permute-done.1.first_ref) | copy-start | bytes 61444
  71.1 0.8 %copy-start.1 = (bf16[32,80,128]{2,1,0:T(8,128)(2,1)}, bf16[32,80,128]{2,1,0:T(8,128)(2,1)S(1)}, u32[]{:S(2)}) copy-start(bf16[32,80,128]{2,1,0:T(8,128)(2,1)S(1)} %all-to-all-done.1.part_ref) | copy-start | bytes 1966084

commit v2 on v1

v2 whole, which is shorter than its diff:
```python
import jax
import jax.numpy as jnp
from jax import lax
from jax.experimental import pallas as pl
from jax.experimental.pallas import tpu as pltpu
from jax.sharding import PartitionSpec as P

KVH = 4
GROUP = 7
HEAD = 128
BLOCK = 256
PLACES = 32
DEVICES = 128
STRIDE = DEVICES // PLACES
ROWS = 2 * GROUP
PAD = 16
QROWS = KVH * ROWS
PROWS = KVH * PAD
CHUNK = PROWS + PAD
LINES = BLOCK * KVH * 2
TILE = 256
META = ROWS
SCORE_UNROLL = 8
WEIGH_UNROLL = 8
LOG2_SCALE = 1.4426950408889634 / HEAD**0.5
HIDDEN = -(2.0**120)
GROUPS = [[STRIDE * i + r for i in range(PLACES)] for r in range(STRIDE)]
NEXT = [(d, (d + 1) % DEVICES) for d in range(DEVICES)]
PREVIOUS = [((d + 1) % DEVICES, d) for d in range(DEVICES)]


def my_member():
    return lax.axis_index("pool") // STRIDE


def iota(shape, dim):
    return lax.broadcasted_iota(jnp.int32, shape, dim)


def pad_matrix(shape, padded_dim):
    padded, plain = iota(shape, padded_dim), iota(shape, 1 - padded_dim)
    hit = (padded % PAD < ROWS) & (padded // PAD * ROWS + padded % PAD == plain)
    return jnp.where(hit, 1.0, 0.0).astype(jnp.bfloat16)


def split3(x):
    hi = x.astype(jnp.bfloat16).astype(jnp.float32)
    rest = x - hi
    mid = rest.astype(jnp.bfloat16).astype(jnp.float32)
    return hi, mid, rest - mid


def pack_kernel(length_ref, table_ref, query_ref, sent_ref, first_ref):
    member = my_member()
    padded = jnp.dot(
        pad_matrix((PROWS, QROWS), 0),
        query_ref[...].astype(jnp.float32).reshape(QROWS, HEAD).astype(jnp.bfloat16),
        preferred_element_type=jnp.float32,
    )
    length = length_ref[0]
    row, lane = iota((PAD, HEAD), 0), iota((PAD, HEAD), 1)
    is_meta = row == META
    length_lanes = jnp.where(lane == 1, length // 128, jnp.where(lane == 2, length % 128, 0))
    head = padded[:PAD]
    rest = padded[PAD:].astype(jnp.bfloat16)

    def chunk_head(place):
        slot = table_ref[place] % PLACES
        meta = jnp.where(lane == 0, slot, length_lanes).astype(jnp.float32)
        return jnp.where(is_meta, meta, head).astype(jnp.bfloat16)

    for i in range(PLACES):
        sent_ref[i, :PAD, :] = chunk_head(lax.rem(i + PLACES - member, PLACES))
        sent_ref[i, PAD:, :] = rest
    first_ref[:PAD, :] = chunk_head(0)
    first_ref[PAD:, :] = rest


def start_scalars(meta_vmem, meta_smem, sem):
    copy = pltpu.make_async_copy(meta_vmem, meta_smem, sem)
    copy.start()
    return copy


def meta_row(rows):
    rows = rows.astype(jnp.float32)
    rows = jnp.where(iota(rows.shape, rows.ndim - 2) == META, rows, 0.0)
    return jnp.sum(rows, axis=-2, keepdims=rows.ndim == 2).astype(jnp.int32)


def meta_rows(peak, total):
    lane = iota((PAD, HEAD), 1)
    rows = jnp.zeros_like(peak)
    for g, part in enumerate((*split3(peak), *split3(total))):
        rows = jnp.where(lane // 8 == g, part, rows)
    return rows.astype(jnp.bfloat16)


def score(query_ref, lines_ref, score_ref, peak_ref, visible):
    lane = iota((PAD, HEAD), 1)
    head = lane % 8 // 2
    limit = 8 * (visible + iota((PAD, HEAD), 0) % 2)
    query = query_ref[...]
    peak = jnp.full((PAD, HEAD), HIDDEN)
    for n in range(LINES // TILE):
        tile = lines_ref[n * TILE : (n + 1) * TILE, :]
        every = lax.dot_general(
            query, tile, (((1,), (1,)), ((), ())), preferred_element_type=jnp.float32
        )
        for half in range(TILE // HEAD):
            part = every[:, half * HEAD : (half + 1) * HEAD]
            own = part[(KVH - 1) * PAD :]
            for k in range(KVH - 1):
                own = jnp.where(head == k, part[k * PAD : (k + 1) * PAD], own)
            at = n * TILE + half * HEAD
            own = jnp.where(lane < limit - at, own, HIDDEN)
            score_ref[:, at : at + HEAD] = own
            peak = jnp.maximum(peak, own)
    for shift in (8, 16, 32, 64):
        peak = jnp.maximum(peak, pltpu.roll(peak, shift, 1))
    peak_ref[...] = peak


def weigh(lines_ref, score_ref, peak_ref, part_ref):
    lane = iota((PAD, HEAD), 1)
    value_of = [
        jnp.where(lane % 8 == 2 * k + 1, 1.0, 0.0).astype(jnp.bfloat16) for k in range(KVH)
    ]
    peak = peak_ref[...]
    total = jnp.zeros((PAD, HEAD), jnp.float32)
    numer = jnp.zeros((PROWS, HEAD), jnp.float32)
    for n in range(LINES // TILE):
        tile = lines_ref[n * TILE : (n + 1) * TILE, :]
        halves = []
        for half in range(TILE // HEAD):
            at = n * TILE + half * HEAD
            unscaled = jnp.exp2((score_ref[:, at : at + HEAD] - peak) * LOG2_SCALE)
            total = total + unscaled
            moved = pltpu.roll(unscaled, 1, 1).astype(jnp.bfloat16)
            halves.append(jnp.concatenate([moved * value_of[k] for k in range(KVH)], axis=0))
        weights = jnp.concatenate(halves, axis=1)
        numer = numer + jnp.dot(weights, tile, preferred_element_type=jnp.float32)
    for shift in (8, 16, 32, 64):
        total = total + pltpu.roll(total, shift, 1)
    part_ref[:PROWS, :] = numer.astype(jnp.bfloat16)
    part_ref[PROWS:, :] = meta_rows(peak, total)


def first_kernel(
    held_ref, pool_ref, part_ref, meta_vmem, meta_smem, sem, scores, peaks, block, load_sem
):
    meta_vmem[...] = jnp.broadcast_to(meta_row(held_ref[:PAD, :]), (8, HEAD))
    start_scalars(meta_vmem, meta_smem, sem).wait()
    load = pltpu.make_async_copy(pool_ref.at[meta_smem[0, 0]], block, load_sem.at[0])
    load.start()
    load.wait()
    score(held_ref, block, scores, peaks, meta_smem[0, 1] * 128 + meta_smem[0, 2] + 1)
    weigh(block, scores, peaks, part_ref)


def attend_kernel(
    held_ref,
    pool_ref,
    _,
    part_ref,
    meta_vmem,
    meta_smem,
    sem,
    scores,
    peaks,
    blocks,
    load_sems,
    owner_at,
    todo,
):
    def load(slot):
        return pltpu.make_async_copy(pool_ref.at[slot], blocks.at[slot], load_sems.at[slot])

    for slot in range(PLACES):
        load(slot).start()
    member = my_member()
    meta_vmem[...] = meta_row(held_ref[:, :PAD, :])
    copy = start_scalars(meta_vmem, meta_smem, sem)
    lane = iota((PAD, HEAD), 1)
    no_numer = jnp.zeros((PROWS, HEAD), jnp.bfloat16)
    no_meta = meta_rows(jnp.full((PAD, HEAD), HIDDEN), jnp.zeros((PAD, HEAD)))
    for i in range(PLACES):
        part_ref[i, :PROWS, :] = no_numer
        part_ref[i, PROWS:, :] = no_meta
        owner_at[i] = jnp.int32(-1)
    copy.wait()

    def visible(i):
        place = lax.rem(member + PLACES - i, PLACES)
        return meta_smem[i, 1] * 128 + meta_smem[i, 2] + 1 - place * BLOCK

    for i in range(PLACES):
        slot = jnp.where(member == i, PLACES, meta_smem[i, 0])
        owner_at[slot] = jnp.where(visible(i) >= 0, i, -1)
    count = jnp.int32(0)
    for slot in range(PLACES):
        todo[count] = jnp.int32(slot)
        count = count + (owner_at[slot] >= 0).astype(jnp.int32)

    def score_one(slot):
        i = owner_at[slot]
        score(held_ref.at[i], blocks.at[slot], scores.at[slot], peaks.at[slot], visible(i))

    def weigh_one(slot):
        weigh(blocks.at[slot], scores.at[slot], peaks.at[slot], part_ref.at[owner_at[slot]])

    for work, unroll in ((score_one, SCORE_UNROLL), (weigh_one, WEIGH_UNROLL)):
        rest = count % unroll
        whole = count // unroll + (rest > unroll // 2).astype(jnp.int32)

        def several(s, width, work=work, unroll=unroll):
            slots = [todo[jnp.minimum(s * unroll + u, count - 1)] for u in range(width)]
            if work is score_one:
                for u in range(width):

                    @pl.when(s * unroll + u < count)
                    def _(u=u):
                        load(slots[u]).wait()

            for slot in slots:
                work(slot)

        def step(s, carry, unroll=unroll, several=several):
            several(s, unroll)
            return carry

        lax.fori_loop(0, whole, step, 0)

        @pl.when((rest > 0) & (rest <= unroll // 2))
        def _(several=several, whole=whole, unroll=unroll):
            several(whole, unroll // 2)

    for slot in range(PLACES):

        @pl.when(owner_at[slot] < 0)
        def _(slot=slot):
            load(slot).wait()


def merge_kernel(part_ref, first_ref, out_ref):
    at, lane = iota((HEAD, HEAD), 0), iota((HEAD, HEAD), 1)
    meta = part_ref[:, PROWS:, :].reshape(PLACES * PAD, HEAD)
    meta_first = first_ref[PROWS:, :]
    merged = []
    for k in range(KVH):
        peak_of = ((at % 8 == 2 * k) & (at < 24)).astype(jnp.float32).astype(jnp.bfloat16)
        total_of = ((at % 8 == 2 * k) & (at >= 24) & (at < 48)).astype(jnp.float32).astype(jnp.bfloat16)

        def spread(rows, of):
            return jnp.dot(rows, of, preferred_element_type=jnp.float32)

        peak = spread(meta, peak_of).reshape(PLACES, PAD, HEAD)
        total = spread(meta, total_of).reshape(PLACES, PAD, HEAD)
        peak_first, total_first = spread(meta_first, peak_of), spread(meta_first, total_of)
        top = jnp.maximum(jnp.max(peak, axis=0), peak_first)
        share = jnp.exp2((peak - top[None]) * LOG2_SCALE)
        share_first = jnp.exp2((peak_first - top) * LOG2_SCALE)
        rows = slice(k * PAD, (k + 1) * PAD)
        numer = part_ref[:, rows, :].astype(jnp.float32)
        numer = jnp.sum(share * numer, axis=0) + share_first * first_ref[rows, :].astype(jnp.float32)
        denom = jnp.sum(share * total, axis=0) + share_first * total_first
        merged.append((numer / denom).astype(jnp.bfloat16))
    merged = jnp.concatenate(merged, axis=0)
    merged = jnp.dot(
        pad_matrix((QROWS, PROWS), 1), merged, preferred_element_type=jnp.float32
    )
    out_ref[...] = merged.reshape(KVH * GROUP, 2, HEAD).astype(jnp.bfloat16)


def vmem(count):
    return [pl.BlockSpec(memory_space=pltpu.VMEM)] * count


def hbm(count):
    return [pl.BlockSpec(memory_space=pltpu.HBM)] * count


def smem(count):
    return [pl.BlockSpec(memory_space=pltpu.SMEM)] * count


def bf16(*shape):
    return jax.ShapeDtypeStruct(shape, jnp.bfloat16)


def pack(lengths, table, query):
    return pl.pallas_call(
        pack_kernel,
        in_specs=smem(2) + vmem(1),
        out_specs=vmem(2),
        out_shape=[bf16(PLACES, PROWS, HEAD), bf16(PROWS, HEAD)],
        compiler_params=pltpu.CompilerParams(vmem_limit_bytes=8 * 2**20),
    )(lengths, table, query)


def scratch(places, rows):
    return [
        pltpu.VMEM((rows, HEAD), jnp.int32),
        pltpu.SMEM((rows, HEAD), jnp.int32),
        pltpu.SemaphoreType.DMA,
        pltpu.VMEM((*places, PAD, LINES), jnp.float32),
        pltpu.VMEM((*places, PAD, HEAD), jnp.float32),
        pltpu.VMEM((*places, LINES, HEAD), jnp.bfloat16),
        pltpu.SemaphoreType.DMA(places or (1,)),
    ]


def attend_first(held, pool):
    return pl.pallas_call(
        first_kernel,
        in_specs=[*vmem(1), *hbm(1)],
        out_specs=vmem(1)[0],
        out_shape=bf16(CHUNK, HEAD),
        scratch_shapes=scratch((), 8),
        compiler_params=pltpu.CompilerParams(vmem_limit_bytes=8 * 2**20),
    )(held, pool)


def attend_blocks(held, pool, part_first):
    return pl.pallas_call(
        attend_kernel,
        in_specs=[*vmem(1), *hbm(1), pl.BlockSpec(memory_space=pl.ANY)],
        out_specs=vmem(1)[0],
        out_shape=bf16(PLACES, CHUNK, HEAD),
        scratch_shapes=[
            *scratch((PLACES,), PLACES),
            pltpu.SMEM((PLACES + 1,), jnp.int32),
            pltpu.SMEM((PLACES,), jnp.int32),
        ],
        compiler_params=pltpu.CompilerParams(vmem_limit_bytes=32 * 2**20),
    )(held, pool, part_first)


def merge(parts, first):
    return pl.pallas_call(
        merge_kernel,
        in_specs=vmem(2),
        out_specs=vmem(1)[0],
        out_shape=bf16(KVH * GROUP, 2, HEAD),
        compiler_params=pltpu.CompilerParams(vmem_limit_bytes=8 * 2**20),
    )(parts, first)


def body(queries, kv_pool, lengths, block_table):
    query = queries.reshape(2, KVH * GROUP, HEAD).swapaxes(0, 1)
    pool = (
        kv_pool.reshape(PLACES, BLOCK, 2, KVH, HEAD)
        .transpose(0, 1, 3, 2, 4)
        .reshape(PLACES, LINES, HEAD)
    )
    pool = pltpu.with_memory_space_constraint(pool, pltpu.HBM)
    sent, first = pack(lengths, block_table, query)
    first = lax.ppermute(first, "pool", NEXT)
    held = lax.all_to_all(sent, "pool", 0, 0, tiled=True, axis_index_groups=GROUPS)
    part_first = attend_first(first, pool)
    parts = attend_blocks(held, pool, part_first)
    part_first = lax.ppermute(part_first, "pool", PREVIOUS)
    parts = lax.all_to_all(parts, "pool", 0, 0, tiled=True, axis_index_groups=GROUPS)
    merged = merge(parts, part_first)
    return (
        merged.swapaxes(0, 1).reshape(1, 2, KVH * GROUP * HEAD)
    )


def solution(mesh):
    placed = (P("pool", None, None), P("pool", None, None, None), P("pool"), P("pool"))
    return jax.shard_map(
        body, mesh=mesh, in_specs=placed, out_specs=P("pool", None, None), check_vma=False
    )
```

time: 76 us -> 58.3 us (0.77)
  local copies, waits for them, and re-layouts: 9.3 us -> 1.36 us
  Pallas kernels: 21.4 us -> 15.8 us
  waiting for transfers between devices: 24.6 us -> 20.2 us
    unnamed x6 -> x4, local copies, waits for them, and re-layouts: 6.62 us -> 1.36 us
    pallas_call x1 -> x2, Pallas kernels: 17.3 us -> 13 us  [the longest x1 10.4 us: attend_blocks(): pl.pallas_call(attend_kernel, in_specs=[*vmem(1), *hbm(1), pl.BlockSpec(m...]
    all_to_all x1, waiting for transfers between devices: 9.07 us -> 6.64 us  [body(): lax.all_to_all(parts, 'pool', 0, 0, tiled=True, axis_index_groups=GROUPS)]
    reshape x3 -> x0, local copies, waits for them, and re-layouts: 2.07 us -> none  [the longest x1 0.73 us: body(): queries.reshape(1, 2, KVH * GROUP, HEAD).transpose(0, 2, 1, 3)]
    ppermute x1, starting transfers between devices: 3.4 us -> 4.91 us  [body(): part_first = lax.ppermute(part_first, 'pool', PREVIOUS)]
    all_to_all x1, waiting for transfers between devices: 1.42 us -> 0.01 us  [body(): lax.all_to_all(sent, 'pool', 0, 0, tiled=True, axis_index_groups=GROUPS)]
    all_to_all x1, starting transfers between devices: 5.32 us -> 4.22 us  [body(): lax.all_to_all(parts, 'pool', 0, 0, tiled=True, axis_index_groups=GROUPS)]
    pallas_call x1, Pallas kernels: 2.39 us -> 1.31 us  [merge(): pl.pallas_call(merge_kernel, in_specs=vmem(2), out_specs=vmem(1)[0], out_...]
  transfers between devices with their start and end apart: 4 -> 4, of which waited for: 4 -> 3; matrix products, arithmetic and copies ran while one was open for 0% -> 0% of each run, Pallas kernels for 0% -> 4%
where the time goes in v2:
time: 58.3 us; the launch traced here: 58.1 us
  waiting for transfers between devices  20.2 us (35%)
  starting transfers between devices  20.1 us (34%)
  Pallas kernels  15.8 us (27%)
  local copies, waits for them, and re-layouts  1.36 us (2%)
  between operations  0.71 us (1%)
    ppermute x1, waiting for transfers between devices, body(): first = lax.ppermute(first, 'pool', NEXT)  12 us
    all_to_all x1, starting transfers between devices, body(): lax.all_to_all(sent, 'pool', 0, 0, tiled=True, axis_index_groups=GROUPS)  10.9 us
    pallas_call x1, Pallas kernels, attend_blocks(): pl.pallas_call(attend_kernel, in_specs=[*vmem(1), *hbm(1), pl.BlockSpec(m...  10.4 us
    all_to_all x1, waiting for transfers between devices, body(): lax.all_to_all(parts, 'pool', 0, 0, tiled=True, axis_index_groups=GROUPS)  6.64 us
    ppermute x1, starting transfers between devices, body(): part_first = lax.ppermute(part_first, 'pool', PREVIOUS)  4.91 us
    all_to_all x1, starting transfers between devices, body(): lax.all_to_all(parts, 'pool', 0, 0, tiled=True, axis_index_groups=GROUPS)  4.22 us
    pallas_call x1, Pallas kernels, attend_first(): pl.pallas_call(first_kernel, in_specs=[*vmem(1), *hbm(1)], out_specs=vmem...  2.58 us
    pallas_call x1, Pallas kernels, pack(): pl.pallas_call(pack_kernel, in_specs=smem(2) + vmem(1), out_specs=vmem(2)...  1.55 us
  transfers between devices with their start and end apart: 4, of which 3 were waited for; matrix products, arithmetic and copies ran while one was open for 0% of the time, Pallas kernels for 4%

profile of v2, /device:TPU:0, one launch (start us, length us, event | category | flops | bytes accessed | tf_op | source)
XLA Modules:
  0.0 58.1 jit_solution(10001608777207627927)
XLA Ops:
  0.7 0.0 copy-start
  0.7 0.7 %copy-done = bf16[1,2,3584]{2,1,0:T(2,128)(2,1)S(1)} copy-done((bf16[1,2,3584]{2,1,0:T(2,128)(2,1)S(1)}, bf16[1,2,3584]{2,1,0:T(2,128)(2,1)}, u32[]{:S(2)}) %copy-start) | copy-done | bytes 14360
  1.4 0.0 copy-start.1
  1.4 0.7 %copy-done.1 = s32[32]{0:T(128)S(1)} copy-done((s32[32]{0:T(128)S(1)}, s32[32]{0:T(128)}, u32[]{:S(2)}) %copy-start.1) | copy-done | bytes 152
  2.0 1.5 %shard_map.46 = (bf16[32,64,128]{2,1,0:T(8,128)(2,1)}, bf16[64,128]{1,0:T(8,128)(2,1)S(1)}) custom-call(s32[1]{0:T(128)S(6)} %copy.6.length_ref, s32[32]{0:T(128)S(1)} %copy-done.1, bf16[28,2,128]{2,1,0:T(2,128)(2,1)S(1)} %bitcast.11), custom_call_target="tpu_custom_call" | custom-call | tf_op jit(solution)/shard_map/pallas_call | solution.py:292
  3.6 10.9 %all-to-all-start = ((bf16[32,64,128]{2,1,0:T(8,128)(2,1)}), bf16[32,64,128]{2,1,0:T(8,128)(2,1)S(1)}, u32[]{:S(2)}, u32[]{:S(2)}) async-start(bf16[32,64,128]{2,1,0:T(8,128)(2,1)} %get-tuple-element.7), calls=%async_computation | async-start | bytes 1048576 | tf_op jit(solution)/shard_map/all_to_all | solution.py:359
  14.5 0.1 collective-permute-start
  14.5 12.0 %collective-permute-done.held_ref = bf16[64,128]{1,0:T(8,128)(2,1)S(1)} collective-permute-done((bf16[64,128]{1,0:T(8,128)(2,1)S(1)}, bf16[64,128]{1,0:T(8,128)(2,1)S(1)}, u32[]{:S(2)}, u32[]{:S(2)}) %collective-permute-start) | collective-permute-done | bytes 16416 | tf_op jit(solution)/shard_map/ppermute | solution.py:358
  26.6 2.6 %shard_map.47._ = bf16[80,128]{1,0:T(8,128)(2,1)S(1)} custom-call(bf16[64,128]{1,0:T(8,128)(2,1)S(1)} %collective-permute-done.held_ref, bf16[32,2048,128]{2,1,0:T(8,128)(2,1)} %bitcast.12), custom_call_target="tpu_custom_call" | custom-call | tf_op jit(solution)/shard_map/pallas_call | solution.py:314
  29.2 0.0 all-to-all-done.held_ref
  29.2 10.4 %shard_map.48 = bf16[32,80,128]{2,1,0:T(8,128)(2,1)} custom-call(bf16[32,64,128]{2,1,0:T(8,128)(2,1)S(1)} %all-to-all-done.held_ref, bf16[32,2048,128]{2,1,0:T(8,128)(2,1)} %bitcast.13, bf16[80,128]{1,0:T(8,128)(2,1)S(1)} %shard_map.47._), custom_call_target="tpu_custom_call" | custom-call | tf_op jit(solution)/shard_map/pallas_call | solution.py:325
  39.6 4.2 %all-to-all-start.1 = ((bf16[32,80,128]{2,1,0:T(8,128)(2,1)}), bf16[32,80,128]{2,1,0:T(8,128)(2,1)S(1)}, u32[]{:S(2)}, u32[]{:S(2)}) async-start(bf16[32,80,128]{2,1,0:T(8,128)(2,1)} %shard_map.48), calls=%async_computation.1 | async-start | bytes 1310720 | tf_op jit(solution)/shard_map/all_to_all | solution.py:363
  43.8 4.9 %collective-permute-start.1 = (bf16[80,128]{1,0:T(8,128)(2,1)S(1)}, bf16[80,128]{1,0:T(8,128)(2,1)S(1)}, u32[]{:S(2)}, u32[]{:S(2)}) collective-permute-start(bf16[80,128]{1,0:T(8,128)(2,1)S(1)} %shard_map.47._), channel_id=1, source_target_pairs={{1,0},{2,1},{3,2},{4,3},{5,4},{6,5},{7,6},{8,7},{9,8},{10,9},{11,1... | collective-permute-start | bytes 61448 | tf_op jit(solution)/shard_map/ppermute | solution.py:362
  48.7 1.5 %collective-permute-done.1.first_ref = bf16[80,128]{1,0:T(8,128)(2,1)S(1)} collective-permute-done((bf16[80,128]{1,0:T(8,128)(2,1)S(1)}, bf16[80,128]{1,0:T(8,128)(2,1)S(1)}, u32[]{:S(2)}, u32[]{:S(2)}) %collective-permute-start.1) | collective-permute-done | bytes 20512 | tf_op jit(solution)/shard_map/ppermute | solution.py:362
  50.2 6.6 %all-to-all-done.1.part_ref = bf16[32,80,128]{2,1,0:T(8,128)(2,1)S(1)} async-done(((bf16[32,80,128]{2,1,0:T(8,128)(2,1)}), bf16[32,80,128]{2,1,0:T(8,128)(2,1)S(1)}, u32[]{:S(2)}, u32[]{:S(2)}) %all-to-all-start.1) | async-done | bytes 655392 | tf_op jit(solution)/shard_map/all_to_all | solution.py:363
  56.8 1.3 %shard_map.49 = bf16[28,2,128]{2,1,0:T(2,128)(2,1)} custom-call(bf16[32,80,128]{2,1,0:T(8,128)(2,1)S(1)} %all-to-all-done.1.part_ref, bf16[80,128]{1,0:T(8,128)(2,1)S(1)} %collective-permute-done.1.first_ref), custom_call_target="tpu_custom_call" | custom-call | tf_op jit(solution)/shard_map/pallas_call | solution.py:340
Async XLA Ops:
  0.7 0.7 %copy-start = (bf16[1,2,3584]{2,1,0:T(2,128)(2,1)S(1)}, bf16[1,2,3584]{2,1,0:T(2,128)(2,1)}, u32[]{:S(2)}) copy-start(bf16[1,2,3584]{2,1,0:T(2,128)(2,1)} %param.4) | copy-start | bytes 43012
  1.4 0.7 %copy-start.1 = (s32[32]{0:T(128)S(1)}, s32[32]{0:T(128)}, u32[]{:S(2)}) copy-start(s32[32]{0:T(128)} %table_ref.1) | copy-start | bytes 388
  3.6 25.6 %all-to-all-start = ((bf16[32,64,128]{2,1,0:T(8,128)(2,1)}), bf16[32,64,128]{2,1,0:T(8,128)(2,1)S(1)}, u32[]{:S(2)}, u32[]{:S(2)}) async-start(bf16[32,64,128]{2,1,0:T(8,128)(2,1)} %get-tuple-element.7), calls=%async_computation | async-start | bytes 1048576 | tf_op jit(solution)/shard_map/all_to_all | solution.py:359
  14.5 12.1 %collective-permute-start = (bf16[64,128]{1,0:T(8,128)(2,1)S(1)}, bf16[64,128]{1,0:T(8,128)(2,1)S(1)}, u32[]{:S(2)}, u32[]{:S(2)}) collective-permute-start(bf16[64,128]{1,0:T(8,128)(2,1)S(1)} %get-tuple-element.8), channel_id=1, source_target_pairs={{0,1},{1,2},{2,3},{3,4},{4,5},{5,6},{6,7},{7,8},{8,9},{9,10},{10,1... | collective-permute-start | bytes 49160 | tf_op jit(solution)/shard_map/ppermute | solution.py:358
  39.6 17.3 %all-to-all-start.1 = ((bf16[32,80,128]{2,1,0:T(8,128)(2,1)}), bf16[32,80,128]{2,1,0:T(8,128)(2,1)S(1)}, u32[]{:S(2)}, u32[]{:S(2)}) async-start(bf16[32,80,128]{2,1,0:T(8,128)(2,1)} %shard_map.48), calls=%async_computation.1 | async-start | bytes 1310720 | tf_op jit(solution)/shard_map/all_to_all | solution.py:363
  43.8 6.4 %collective-permute-start.1 = (bf16[80,128]{1,0:T(8,128)(2,1)S(1)}, bf16[80,128]{1,0:T(8,128)(2,1)S(1)}, u32[]{:S(2)}, u32[]{:S(2)}) collective-permute-start(bf16[80,128]{1,0:T(8,128)(2,1)S(1)} %shard_map.47._), channel_id=1, source_target_pairs={{1,0},{2,1},{3,2},{4,3},{5,4},{6,5},{7,6},{8,7},{9,8},{10,9},{11,1... | collective-permute-start | bytes 61448 | tf_op jit(solution)/shard_map/ppermute | solution.py:362

commit v3 on v2

--- a/solution.py
+++ b/solution.py
@@ -20,7 +20,7 @@
 LINES = BLOCK * KVH * 2
 TILE = 256
 META = ROWS
-SCORE_UNROLL = 8
+SCORE_UNROLL = 4
 WEIGH_UNROLL = 8
 LOG2_SCALE = 1.4426950408889634 / HEAD**0.5
 HIDDEN = -(2.0**120)
@@ -50,8 +50,18 @@
     return hi, mid, rest - mid
 
 
-def pack_kernel(length_ref, table_ref, query_ref, sent_ref, first_ref):
+def pack_kernel(
+    length_ref, table_hbm, query_hbm, sent_ref, first_ref, table_ref, query_ref, sems
+):
+    copies = [
+        pltpu.make_async_copy(table_hbm, table_ref, sems.at[0]),
+        pltpu.make_async_copy(query_hbm, query_ref, sems.at[1]),
+    ]
+    for copy in copies:
+        copy.start()
     member = my_member()
+    for copy in copies:
+        copy.wait()
     padded = jnp.dot(
         pad_matrix((PROWS, QROWS), 0),
         query_ref[...].astype(jnp.float32).reshape(QROWS, HEAD).astype(jnp.bfloat16),
@@ -280,10 +290,6 @@
     return [pl.BlockSpec(memory_space=pltpu.HBM)] * count
 
 
-def smem(count):
-    return [pl.BlockSpec(memory_space=pltpu.SMEM)] * count
-
-
 def bf16(*shape):
     return jax.ShapeDtypeStruct(shape, jnp.bfloat16)
 
@@ -291,9 +297,14 @@
 def pack(lengths, table, query):
     return pl.pallas_call(
         pack_kernel,
-        in_specs=smem(2) + vmem(1),
+        in_specs=[pl.BlockSpec(memory_space=pltpu.SMEM), *hbm(2)],
         out_specs=vmem(2),
         out_shape=[bf16(PLACES, PROWS, HEAD), bf16(PROWS, HEAD)],
+        scratch_shapes=[
+            pltpu.SMEM((PLACES,), jnp.int32),
+            pltpu.VMEM((KVH * GROUP, 2, HEAD), jnp.bfloat16),
+            pltpu.SemaphoreType.DMA((2,)),
+        ],
         compiler_params=pltpu.CompilerParams(vmem_limit_bytes=8 * 2**20),
     )(lengths, table, query)
 
@@ -321,7 +332,7 @@
     )(held, pool)
 
 
-def attend_blocks(held, pool, part_first):
+def attend_blocks(held, pool, first):
     return pl.pallas_call(
         attend_kernel,
         in_specs=[*vmem(1), *hbm(1), pl.BlockSpec(memory_space=pl.ANY)],
@@ -333,7 +344,7 @@
             pltpu.SMEM((PLACES,), jnp.int32),
         ],
         compiler_params=pltpu.CompilerParams(vmem_limit_bytes=32 * 2**20),
-    )(held, pool, part_first)
+    )(held, pool, first)
 
 
 def merge(parts, first):
@@ -354,12 +365,14 @@
         .reshape(PLACES, LINES, HEAD)
     )
     pool = pltpu.with_memory_space_constraint(pool, pltpu.HBM)
-    sent, first = pack(lengths, block_table, query)
+    sent, first = pack(
+        lengths,
+        *(pltpu.with_memory_space_constraint(a, pltpu.HBM) for a in (block_table, query)),
+    )
     first = lax.ppermute(first, "pool", NEXT)
     held = lax.all_to_all(sent, "pool", 0, 0, tiled=True, axis_index_groups=GROUPS)
-    part_first = attend_first(first, pool)
-    parts = attend_blocks(held, pool, part_first)
-    part_first = lax.ppermute(part_first, "pool", PREVIOUS)
+    parts = attend_blocks(held, pool, first)
+    part_first = lax.ppermute(attend_first(first, pool), "pool", PREVIOUS)
     parts = lax.all_to_all(parts, "pool", 0, 0, tiled=True, axis_index_groups=GROUPS)
     merged = merge(parts, part_first)
     return (

time: 58.3 us -> 57.1 us (0.979)
  local copies, waits for them, and re-layouts: 1.36 us -> 0 us
    all_to_all x1, waiting for transfers between devices: 6.64 us -> 4.95 us  [body(): lax.all_to_all(parts, 'pool', 0, 0, tiled=True, axis_index_groups=GROUPS)]
    all_to_all x1, waiting for transfers between devices: 0.01 us -> 1.42 us  [body(): lax.all_to_all(sent, 'pool', 0, 0, tiled=True, axis_index_groups=GROUPS)]
    unnamed x4 -> x0, local copies, waits for them, and re-layouts: 1.36 us -> none
  transfers between devices with their start and end apart: 4 -> 4, of which waited for: 3 -> 4; matrix products, arithmetic and copies ran while one was open for 0% -> 0% of each run, Pallas kernels for 4% -> 5%
where the time goes in v3:
time: 57.1 us; the launch traced here: 56.5 us
  waiting for transfers between devices  19.9 us (35%)
  starting transfers between devices  19.7 us (35%)
  Pallas kernels  16.2 us (28%)
  between operations  0.7 us (1%)
    ppermute x1, waiting for transfers between devices, body(): first = lax.ppermute(first, 'pool', NEXT)  12 us
    all_to_all x1, starting transfers between devices, body(): lax.all_to_all(sent, 'pool', 0, 0, tiled=True, axis_index_groups=GROUPS)  10.9 us
    pallas_call x1, Pallas kernels, attend_blocks(): pl.pallas_call(attend_kernel, in_specs=[*vmem(1), *hbm(1), pl.BlockSpec(m...  10.6 us
    all_to_all x1, waiting for transfers between devices, body(): lax.all_to_all(parts, 'pool', 0, 0, tiled=True, axis_index_groups=GROUPS)  4.95 us
    ppermute x1, starting transfers between devices, body(): part_first = lax.ppermute(attend_first(first, pool), 'pool', PREVIOUS)  4.79 us
    all_to_all x1, starting transfers between devices, body(): lax.all_to_all(parts, 'pool', 0, 0, tiled=True, axis_index_groups=GROUPS)  3.91 us
    pallas_call x1, Pallas kernels, attend_first(): pl.pallas_call(first_kernel, in_specs=[*vmem(1), *hbm(1)], out_specs=vmem...  2.59 us
    pallas_call x1, Pallas kernels, pack(): pl.pallas_call(pack_kernel, in_specs=[pl.BlockSpec(memory_space=pltpu.SME...  1.73 us
  transfers between devices with their start and end apart: 4, of which 4 were waited for; matrix products, arithmetic and copies ran while one was open for 0% of the time, Pallas kernels for 5%

profile of v3, /device:TPU:0, one launch (start us, length us, event | category | flops | bytes accessed | tf_op | source)
XLA Modules:
  0.0 56.5 jit_solution(17513414151520451532)
XLA Ops:
  0.7 1.7 %shard_map.46 = (bf16[32,64,128]{2,1,0:T(8,128)(2,1)}, bf16[64,128]{1,0:T(8,128)(2,1)S(1)}) custom-call(s32[1]{0:T(128)S(6)} %copy.6.length_ref, s32[32]{0:T(128)} %table_hbm.1, bf16[28,2,128]{2,1,0:T(2,128)(2,1)} %bitcast.13), custom_call_target="tpu_custom_call" | custom-call | tf_op jit(solution)/shard_map/pallas_call | solution.py:298
  2.4 10.9 %all-to-all-start = ((bf16[32,64,128]{2,1,0:T(8,128)(2,1)}), bf16[32,64,128]{2,1,0:T(8,128)(2,1)S(1)}, u32[]{:S(2)}, u32[]{:S(2)}) async-start(bf16[32,64,128]{2,1,0:T(8,128)(2,1)} %get-tuple-element.7), calls=%async_computation | async-start | bytes 1048576 | tf_op jit(solution)/shard_map/all_to_all | solution.py:373
  13.3 0.1 collective-permute-start
  13.4 12.0 %collective-permute-done._.held_ref = bf16[64,128]{1,0:T(8,128)(2,1)S(1)} collective-permute-done((bf16[64,128]{1,0:T(8,128)(2,1)S(1)}, bf16[64,128]{1,0:T(8,128)(2,1)S(1)}, u32[]{:S(2)}, u32[]{:S(2)}) %collective-permute-start) | collective-permute-done | bytes 16416 | tf_op jit(solution)/shard_map/ppermute | solution.py:372
  25.4 1.4 %all-to-all-done.held_ref = bf16[32,64,128]{2,1,0:T(8,128)(2,1)S(1)} async-done(((bf16[32,64,128]{2,1,0:T(8,128)(2,1)}), bf16[32,64,128]{2,1,0:T(8,128)(2,1)S(1)}, u32[]{:S(2)}, u32[]{:S(2)}) %all-to-all-start) | async-done | bytes 524320 | tf_op jit(solution)/shard_map/all_to_all | solution.py:373
  26.8 10.6 %shard_map.47 = bf16[32,80,128]{2,1,0:T(8,128)(2,1)} custom-call(bf16[32,64,128]{2,1,0:T(8,128)(2,1)S(1)} %all-to-all-done.held_ref, bf16[32,2048,128]{2,1,0:T(8,128)(2,1)} %bitcast.11, bf16[64,128]{1,0:T(8,128)(2,1)S(1)} %collective-permute-done._.held_ref), custom_call_target="tpu_custom_call" | custom-call | tf_op jit(solution)/shard_map/pallas_call | solution.py:336
  37.4 3.9 %all-to-all-start.1 = ((bf16[32,80,128]{2,1,0:T(8,128)(2,1)}), bf16[32,80,128]{2,1,0:T(8,128)(2,1)S(1)}, u32[]{:S(2)}, u32[]{:S(2)}) async-start(bf16[32,80,128]{2,1,0:T(8,128)(2,1)} %shard_map.47), calls=%async_computation.1 | async-start | bytes 1310720 | tf_op jit(solution)/shard_map/all_to_all | solution.py:376
  41.4 2.6 %shard_map.48 = bf16[80,128]{1,0:T(8,128)(2,1)S(1)} custom-call(bf16[64,128]{1,0:T(8,128)(2,1)S(1)} %collective-permute-done._.held_ref, bf16[32,2048,128]{2,1,0:T(8,128)(2,1)} %bitcast.12), custom_call_target="tpu_custom_call" | custom-call | tf_op jit(solution)/shard_map/pallas_call | solution.py:325
  44.0 4.8 %collective-permute-start.1 = (bf16[80,128]{1,0:T(8,128)(2,1)S(1)}, bf16[80,128]{1,0:T(8,128)(2,1)S(1)}, u32[]{:S(2)}, u32[]{:S(2)}) collective-permute-start(bf16[80,128]{1,0:T(8,128)(2,1)S(1)} %shard_map.48), channel_id=1, source_target_pairs={{1,0},{2,1},{3,2},{4,3},{5,4},{6,5},{7,6},{8,7},{9,8},{10,9},{11,1... | collective-permute-start | bytes 61448 | tf_op jit(solution)/shard_map/ppermute | solution.py:375
  48.7 1.5 %collective-permute-done.1.first_ref = bf16[80,128]{1,0:T(8,128)(2,1)S(1)} collective-permute-done((bf16[80,128]{1,0:T(8,128)(2,1)S(1)}, bf16[80,128]{1,0:T(8,128)(2,1)S(1)}, u32[]{:S(2)}, u32[]{:S(2)}) %collective-permute-start.1) | collective-permute-done | bytes 20512 | tf_op jit(solution)/shard_map/ppermute | solution.py:375
  50.2 4.9 %all-to-all-done.1.part_ref = bf16[32,80,128]{2,1,0:T(8,128)(2,1)S(1)} async-done(((bf16[32,80,128]{2,1,0:T(8,128)(2,1)}), bf16[32,80,128]{2,1,0:T(8,128)(2,1)S(1)}, u32[]{:S(2)}, u32[]{:S(2)}) %all-to-all-start.1) | async-done | bytes 655392 | tf_op jit(solution)/shard_map/all_to_all | solution.py:376
  55.2 1.3 %shard_map.49 = bf16[28,2,128]{2,1,0:T(2,128)(2,1)} custom-call(bf16[32,80,128]{2,1,0:T(8,128)(2,1)S(1)} %all-to-all-done.1.part_ref, bf16[80,128]{1,0:T(8,128)(2,1)S(1)} %collective-permute-done.1.first_ref), custom_call_target="tpu_custom_call" | custom-call | tf_op jit(solution)/shard_map/pallas_call | solution.py:351
Async XLA Ops:
  2.4 24.4 %all-to-all-start = ((bf16[32,64,128]{2,1,0:T(8,128)(2,1)}), bf16[32,64,128]{2,1,0:T(8,128)(2,1)S(1)}, u32[]{:S(2)}, u32[]{:S(2)}) async-start(bf16[32,64,128]{2,1,0:T(8,128)(2,1)} %get-tuple-element.7), calls=%async_computation | async-start | bytes 1048576 | tf_op jit(solution)/shard_map/all_to_all | solution.py:373
  13.3 12.1 %collective-permute-start = (bf16[64,128]{1,0:T(8,128)(2,1)S(1)}, bf16[64,128]{1,0:T(8,128)(2,1)S(1)}, u32[]{:S(2)}, u32[]{:S(2)}) collective-permute-start(bf16[64,128]{1,0:T(8,128)(2,1)S(1)} %get-tuple-element.8), channel_id=1, source_target_pairs={{0,1},{1,2},{2,3},{3,4},{4,5},{5,6},{6,7},{7,8},{8,9},{9,10},{10,1... | collective-permute-start | bytes 49160 | tf_op jit(solution)/shard_map/ppermute | solution.py:372
  37.4 17.7 %all-to-all-start.1 = ((bf16[32,80,128]{2,1,0:T(8,128)(2,1)}), bf16[32,80,128]{2,1,0:T(8,128)(2,1)S(1)}, u32[]{:S(2)}, u32[]{:S(2)}) async-start(bf16[32,80,128]{2,1,0:T(8,128)(2,1)} %shard_map.47), calls=%async_computation.1 | async-start | bytes 1310720 | tf_op jit(solution)/shard_map/all_to_all | solution.py:376
  44.0 6.3 %collective-permute-start.1 = (bf16[80,128]{1,0:T(8,128)(2,1)S(1)}, bf16[80,128]{1,0:T(8,128)(2,1)S(1)}, u32[]{:S(2)}, u32[]{:S(2)}) collective-permute-start(bf16[80,128]{1,0:T(8,128)(2,1)S(1)} %shard_map.48), channel_id=1, source_target_pairs={{1,0},{2,1},{3,2},{4,3},{5,4},{6,5},{7,6},{8,7},{9,8},{10,9},{11,1... | collective-permute-start | bytes 61448 | tf_op jit(solution)/shard_map/ppermute | solution.py:375

commit v4 on v3

--- a/solution.py
+++ b/solution.py
@@ -168,9 +168,15 @@
     weigh(block, scores, peaks, part_ref)
 
 
+def empty_kernel(part_ref):
+    part_ref[:PROWS, :] = jnp.zeros((PROWS, HEAD), jnp.bfloat16)
+    part_ref[PROWS:, :] = meta_rows(jnp.full((PAD, HEAD), HIDDEN), jnp.zeros((PAD, HEAD)))
+
+
 def attend_kernel(
     held_ref,
     pool_ref,
+    empty_ref,
     _,
     part_ref,
     meta_vmem,
@@ -191,12 +197,9 @@
     member = my_member()
     meta_vmem[...] = meta_row(held_ref[:, :PAD, :])
     copy = start_scalars(meta_vmem, meta_smem, sem)
-    lane = iota((PAD, HEAD), 1)
-    no_numer = jnp.zeros((PROWS, HEAD), jnp.bfloat16)
-    no_meta = meta_rows(jnp.full((PAD, HEAD), HIDDEN), jnp.zeros((PAD, HEAD)))
+    empty = empty_ref[...]
     for i in range(PLACES):
-        part_ref[i, :PROWS, :] = no_numer
-        part_ref[i, PROWS:, :] = no_meta
+        part_ref[i] = empty
         owner_at[i] = jnp.int32(-1)
     copy.wait()
 
@@ -332,10 +335,20 @@
     )(held, pool)
 
 
-def attend_blocks(held, pool, first):
+def empty_part():
+    return pl.pallas_call(
+        empty_kernel,
+        out_specs=vmem(1)[0],
+        out_shape=bf16(CHUNK, HEAD),
+        compiler_params=pltpu.CompilerParams(vmem_limit_bytes=2 * 2**20),
+        cost_estimate=pl.CostEstimate(flops=10**10, transcendentals=0, bytes_accessed=2**15),
+    )()
+
+
+def attend_blocks(held, pool, empty, first):
     return pl.pallas_call(
         attend_kernel,
-        in_specs=[*vmem(1), *hbm(1), pl.BlockSpec(memory_space=pl.ANY)],
+        in_specs=[*vmem(1), *hbm(1), *vmem(1), pl.BlockSpec(memory_space=pl.ANY)],
         out_specs=vmem(1)[0],
         out_shape=bf16(PLACES, CHUNK, HEAD),
         scratch_shapes=[
@@ -344,7 +357,7 @@
             pltpu.SMEM((PLACES,), jnp.int32),
         ],
         compiler_params=pltpu.CompilerParams(vmem_limit_bytes=32 * 2**20),
-    )(held, pool, first)
+    )(held, pool, empty, first)
 
 
 def merge(parts, first):
@@ -371,7 +384,7 @@
     )
     first = lax.ppermute(first, "pool", NEXT)
     held = lax.all_to_all(sent, "pool", 0, 0, tiled=True, axis_index_groups=GROUPS)
-    parts = attend_blocks(held, pool, first)
+    parts = attend_blocks(held, pool, empty_part(), first)
     part_first = lax.ppermute(attend_first(first, pool), "pool", PREVIOUS)
     parts = lax.all_to_all(parts, "pool", 0, 0, tiled=True, axis_index_groups=GROUPS)
     merged = merge(parts, part_first)

time: 57.1 us -> 59.2 us (1.037)
  starting transfers between devices: 19.7 us -> 21.7 us
    all_to_all x1, waiting for transfers between devices: 1.42 us -> 14.6 us  [body(): lax.all_to_all(sent, 'pool', 0, 0, tiled=True, axis_index_groups=GROUPS)]
    ppermute x1, waiting for transfers between devices: 12 us -> 0.01 us  [body(): first = lax.ppermute(first, 'pool', NEXT)]
    ppermute x1, starting transfers between devices: 4.79 us -> 6.68 us  [body(): part_first = lax.ppermute(attend_first(first, pool), 'pool', PREVIOUS)]
    all_to_all x1, waiting for transfers between devices: 4.95 us -> 3.59 us  [body(): lax.all_to_all(parts, 'pool', 0, 0, tiled=True, axis_index_groups=GROUPS)]
    pallas_call x1 -> x2, Pallas kernels: 10.6 us -> 10.8 us  [the longest x1 10.8 us: attend_blocks(): pl.pallas_call(attend_kernel, in_specs=[*vmem(1), *hbm(1), *vmem(1), pl.B...]
  transfers between devices with their start and end apart: 4 -> 4, of which waited for: 4 -> 3; matrix products, arithmetic and copies ran while one was open for 0% -> 0% of each run, Pallas kernels for 5% -> 4%
where the time goes in v4:
time: 59.2 us; the launch traced here: 58.6 us
  starting transfers between devices  21.7 us (37%)
  waiting for transfers between devices  19.7 us (33%)
  Pallas kernels  16.4 us (28%)
  between operations  0.72 us (1%)
    all_to_all x1, waiting for transfers between devices, body(): lax.all_to_all(sent, 'pool', 0, 0, tiled=True, axis_index_groups=GROUPS)  14.6 us
    all_to_all x1, starting transfers between devices, body(): lax.all_to_all(sent, 'pool', 0, 0, tiled=True, axis_index_groups=GROUPS)  10.9 us
    pallas_call x1, Pallas kernels, attend_blocks(): pl.pallas_call(attend_kernel, in_specs=[*vmem(1), *hbm(1), *vmem(1), pl.B...  10.8 us
    ppermute x1, starting transfers between devices, body(): part_first = lax.ppermute(attend_first(first, pool), 'pool', PREVIOUS)  6.68 us
    all_to_all x1, starting transfers between devices, body(): lax.all_to_all(parts, 'pool', 0, 0, tiled=True, axis_index_groups=GROUPS)  4.07 us
    all_to_all x1, waiting for transfers between devices, body(): lax.all_to_all(parts, 'pool', 0, 0, tiled=True, axis_index_groups=GROUPS)  3.59 us
    pallas_call x1, Pallas kernels, attend_first(): pl.pallas_call(first_kernel, in_specs=[*vmem(1), *hbm(1)], out_specs=vmem...  2.59 us
    pallas_call x1, Pallas kernels, pack(): pl.pallas_call(pack_kernel, in_specs=[pl.BlockSpec(memory_space=pltpu.SME...  1.73 us
  transfers between devices with their start and end apart: 4, of which 3 were waited for; matrix products, arithmetic and copies ran while one was open for 0% of the time, Pallas kernels for 4%

profile of v4, /device:TPU:0, one launch (start us, length us, event | category | flops | bytes accessed | tf_op | source)
XLA Modules:
  0.0 58.6 jit_solution(5973785782276733965)
XLA Ops:
  0.7 1.7 %shard_map.46 = (bf16[32,64,128]{2,1,0:T(8,128)(2,1)}, bf16[64,128]{1,0:T(8,128)(2,1)S(1)}) custom-call(s32[1]{0:T(128)S(6)} %copy.6.length_ref, s32[32]{0:T(128)} %table_hbm.1, bf16[28,2,128]{2,1,0:T(2,128)(2,1)} %bitcast.13), custom_call_target="tpu_custom_call" | custom-call | tf_op jit(solution)/shard_map/pallas_call | solution.py:301
  2.4 0.1 collective-permute-start
  2.5 10.9 %all-to-all-start = ((bf16[32,64,128]{2,1,0:T(8,128)(2,1)}), bf16[32,64,128]{2,1,0:T(8,128)(2,1)S(1)}, u32[]{:S(2)}, u32[]{:S(2)}) async-start(bf16[32,64,128]{2,1,0:T(8,128)(2,1)} %get-tuple-element.7), calls=%async_computation | async-start | bytes 1048576 | tf_op jit(solution)/shard_map/all_to_all | solution.py:386
  13.4 0.0 collective-permute-done._.held_ref
  13.4 14.6 %all-to-all-done.held_ref = bf16[32,64,128]{2,1,0:T(8,128)(2,1)S(1)} async-done(((bf16[32,64,128]{2,1,0:T(8,128)(2,1)}), bf16[32,64,128]{2,1,0:T(8,128)(2,1)S(1)}, u32[]{:S(2)}, u32[]{:S(2)}) %all-to-all-start) | async-done | bytes 524320 | tf_op jit(solution)/shard_map/all_to_all | solution.py:386
  28.0 10.8 %shard_map.48 = bf16[32,80,128]{2,1,0:T(8,128)(2,1)} custom-call(bf16[32,64,128]{2,1,0:T(8,128)(2,1)S(1)} %all-to-all-done.held_ref, bf16[32,2048,128]{2,1,0:T(8,128)(2,1)} %bitcast.11, bf16[80,128]{1,0:T(8,128)(2,1)S(1)} %shard_map.47.empty_ref, bf16[64,128]{1,0:T(8,128)(2,1)S(1)} %collective-permute-done._.held_ref), custom_call_target="tpu_custom_call" | custom-call | tf_op jit(solution)/shard_map/pallas_call | solution.py:349
  38.8 4.1 %all-to-all-start.1 = ((bf16[32,80,128]{2,1,0:T(8,128)(2,1)}), bf16[32,80,128]{2,1,0:T(8,128)(2,1)S(1)}, u32[]{:S(2)}, u32[]{:S(2)}) async-start(bf16[32,80,128]{2,1,0:T(8,128)(2,1)} %shard_map.48), calls=%async_computation.1 | async-start | bytes 1310720 | tf_op jit(solution)/shard_map/all_to_all | solution.py:389
  42.9 2.6 %shard_map.49 = bf16[80,128]{1,0:T(8,128)(2,1)S(1)} custom-call(bf16[64,128]{1,0:T(8,128)(2,1)S(1)} %collective-permute-done._.held_ref, bf16[32,2048,128]{2,1,0:T(8,128)(2,1)} %bitcast.12), custom_call_target="tpu_custom_call" | custom-call | tf_op jit(solution)/shard_map/pallas_call | solution.py:328
  45.5 6.7 %collective-permute-start.1 = (bf16[80,128]{1,0:T(8,128)(2,1)S(1)}, bf16[80,128]{1,0:T(8,128)(2,1)S(1)}, u32[]{:S(2)}, u32[]{:S(2)}) collective-permute-start(bf16[80,128]{1,0:T(8,128)(2,1)S(1)} %shard_map.49), channel_id=1, source_target_pairs={{1,0},{2,1},{3,2},{4,3},{5,4},{6,5},{7,6},{8,7},{9,8},{10,9},{11,1... | collective-permute-start | bytes 61448 | tf_op jit(solution)/shard_map/ppermute | solution.py:388
  52.2 1.5 %collective-permute-done.1.first_ref = bf16[80,128]{1,0:T(8,128)(2,1)S(1)} collective-permute-done((bf16[80,128]{1,0:T(8,128)(2,1)S(1)}, bf16[80,128]{1,0:T(8,128)(2,1)S(1)}, u32[]{:S(2)}, u32[]{:S(2)}) %collective-permute-start.1) | collective-permute-done | bytes 20512 | tf_op jit(solution)/shard_map/ppermute | solution.py:388
  53.7 3.6 %all-to-all-done.1.part_ref = bf16[32,80,128]{2,1,0:T(8,128)(2,1)S(1)} async-done(((bf16[32,80,128]{2,1,0:T(8,128)(2,1)}), bf16[32,80,128]{2,1,0:T(8,128)(2,1)S(1)}, u32[]{:S(2)}, u32[]{:S(2)}) %all-to-all-start.1) | async-done | bytes 655392 | tf_op jit(solution)/shard_map/all_to_all | solution.py:389
  57.2 1.3 %shard_map.50 = bf16[28,2,128]{2,1,0:T(2,128)(2,1)} custom-call(bf16[32,80,128]{2,1,0:T(8,128)(2,1)S(1)} %all-to-all-done.1.part_ref, bf16[80,128]{1,0:T(8,128)(2,1)S(1)} %collective-permute-done.1.first_ref), custom_call_target="tpu_custom_call" | custom-call | tf_op jit(solution)/shard_map/pallas_call | solution.py:364
  (1 shorter events, 0.0 us)
Async XLA Ops:
  2.4 11.0 %collective-permute-start = (bf16[64,128]{1,0:T(8,128)(2,1)S(1)}, bf16[64,128]{1,0:T(8,128)(2,1)S(1)}, u32[]{:S(2)}, u32[]{:S(2)}) collective-permute-start(bf16[64,128]{1,0:T(8,128)(2,1)S(1)} %get-tuple-element.8), channel_id=1, source_target_pairs={{0,1},{1,2},{2,3},{3,4},{4,5},{5,6},{6,7},{7,8},{8,9},{9,10},{10,1... | collective-permute-start | bytes 49160 | tf_op jit(solution)/shard_map/ppermute | solution.py:385
  2.5 25.6 %all-to-all-start = ((bf16[32,64,128]{2,1,0:T(8,128)(2,1)}), bf16[32,64,128]{2,1,0:T(8,128)(2,1)S(1)}, u32[]{:S(2)}, u32[]{:S(2)}) async-start(bf16[32,64,128]{2,1,0:T(8,128)(2,1)} %get-tuple-element.7), calls=%async_computation | async-start | bytes 1048576 | tf_op jit(solution)/shard_map/all_to_all | solution.py:386
  38.8 18.4 %all-to-all-start.1 = ((bf16[32,80,128]{2,1,0:T(8,128)(2,1)}), bf16[32,80,128]{2,1,0:T(8,128)(2,1)S(1)}, u32[]{:S(2)}, u32[]{:S(2)}) async-start(bf16[32,80,128]{2,1,0:T(8,128)(2,1)} %shard_map.48), calls=%async_computation.1 | async-start | bytes 1310720 | tf_op jit(solution)/shard_map/all_to_all | solution.py:389
  45.5 8.2 %collective-permute-start.1 = (bf16[80,128]{1,0:T(8,128)(2,1)S(1)}, bf16[80,128]{1,0:T(8,128)(2,1)S(1)}, u32[]{:S(2)}, u32[]{:S(2)}) collective-permute-start(bf16[80,128]{1,0:T(8,128)(2,1)S(1)} %shard_map.49), channel_id=1, source_target_pairs={{1,0},{2,1},{3,2},{4,3},{5,4},{6,5},{7,6},{8,7},{9,8},{10,9},{11,1... | collective-permute-start | bytes 61448 | tf_op jit(solution)/shard_map/ppermute | solution.py:388

commit v5 on v3

--- a/solution.py
+++ b/solution.py
@@ -16,7 +16,6 @@
 PAD = 16
 QROWS = KVH * ROWS
 PROWS = KVH * PAD
-CHUNK = PROWS + PAD
 LINES = BLOCK * KVH * 2
 TILE = 256
 META = ROWS
@@ -98,12 +97,17 @@
     return jnp.sum(rows, axis=-2, keepdims=rows.ndim == 2).astype(jnp.int32)
 
 
-def meta_rows(peak, total):
-    lane = iota((PAD, HEAD), 1)
-    rows = jnp.zeros_like(peak)
-    for g, part in enumerate((*split3(peak), *split3(total))):
-        rows = jnp.where(lane // 8 == g, part, rows)
-    return rows.astype(jnp.bfloat16)
+def store_part(part_ref, numer, peak, total):
+    row, lane = iota((PAD, HEAD), 0), iota((PAD, HEAD), 1)
+    peak, total = (
+        jnp.sum(jnp.where(lane // 8 == row, x, 0.0), axis=0, keepdims=True) for x in (peak, total)
+    )
+    parts = (*split3(peak), *split3(total))
+    for k in range(KVH):
+        rows = numer[k * PAD : (k + 1) * PAD]
+        for at, part in enumerate(parts[2 * k : 2 * k + 2]):
+            rows = jnp.where(row == ROWS + at, part, rows)
+        part_ref[k * PAD : (k + 1) * PAD, :] = rows.astype(jnp.bfloat16)
 
 
 def score(query_ref, lines_ref, score_ref, peak_ref, visible):
@@ -152,8 +156,7 @@
         numer = numer + jnp.dot(weights, tile, preferred_element_type=jnp.float32)
     for shift in (8, 16, 32, 64):
         total = total + pltpu.roll(total, shift, 1)
-    part_ref[:PROWS, :] = numer.astype(jnp.bfloat16)
-    part_ref[PROWS:, :] = meta_rows(peak, total)
+    store_part(part_ref, numer, peak, total)
 
 
 def first_kernel(
@@ -191,12 +194,9 @@
     member = my_member()
     meta_vmem[...] = meta_row(held_ref[:, :PAD, :])
     copy = start_scalars(meta_vmem, meta_smem, sem)
-    lane = iota((PAD, HEAD), 1)
-    no_numer = jnp.zeros((PROWS, HEAD), jnp.bfloat16)
-    no_meta = meta_rows(jnp.full((PAD, HEAD), HIDDEN), jnp.zeros((PAD, HEAD)))
+    empty = jnp.where(iota((PROWS, HEAD), 0) == ROWS, HIDDEN, 0.0).astype(jnp.bfloat16)
     for i in range(PLACES):
-        part_ref[i, :PROWS, :] = no_numer
-        part_ref[i, PROWS:, :] = no_meta
+        part_ref[i] = empty
         owner_at[i] = jnp.int32(-1)
     copy.wait()
 
@@ -253,28 +253,37 @@
 
 
 def merge_kernel(part_ref, first_ref, out_ref):
-    at, lane = iota((HEAD, HEAD), 0), iota((HEAD, HEAD), 1)
-    meta = part_ref[:, PROWS:, :].reshape(PLACES * PAD, HEAD)
-    meta_first = first_ref[PROWS:, :]
+    row, lane = iota((PAD, HEAD), 0), iota((PAD, HEAD), 1)
+
+    def heads(ref):
+        return [
+            ref[..., k * PAD : (k + 1) * PAD, :].astype(jnp.float32) for k in range(KVH)
+        ]
+
+    def peak_and_total(numer):
+        peak = jnp.where(row >= ROWS, numer[0], 0.0) + jnp.where(row == ROWS, numer[1], 0.0)
+        total = jnp.where(row > ROWS, numer[1], 0.0) + jnp.where(row >= ROWS, numer[2], 0.0)
+        keep = peak.ndim == 2
+        return (jnp.sum(x, axis=-2, keepdims=keep) for x in (peak, total))
+
+    numer, numer_first = heads(part_ref), heads(first_ref)
+    peak, total = peak_and_total(numer)
+    peak_first, total_first = peak_and_total(numer_first)
+    top = jnp.maximum(jnp.max(peak, axis=0, keepdims=True), peak_first)
+    share = jnp.exp2((peak - top) * LOG2_SCALE)
+    share_first = jnp.exp2((peak_first - top) * LOG2_SCALE)
+    denom = jnp.sum(share * total, axis=0, keepdims=True) + share_first * total_first
+    share, share_first = share / denom, share_first / denom
     merged = []
     for k in range(KVH):
-        peak_of = ((at % 8 == 2 * k) & (at < 24)).astype(jnp.float32).astype(jnp.bfloat16)
-        total_of = ((at % 8 == 2 * k) & (at >= 24) & (at < 48)).astype(jnp.float32).astype(jnp.bfloat16)
-
-        def spread(rows, of):
-            return jnp.dot(rows, of, preferred_element_type=jnp.float32)
-
-        peak = spread(meta, peak_of).reshape(PLACES, PAD, HEAD)
-        total = spread(meta, total_of).reshape(PLACES, PAD, HEAD)
-        peak_first, total_first = spread(meta_first, peak_of), spread(meta_first, total_of)
-        top = jnp.maximum(jnp.max(peak, axis=0), peak_first)
-        share = jnp.exp2((peak - top[None]) * LOG2_SCALE)
-        share_first = jnp.exp2((peak_first - top) * LOG2_SCALE)
-        rows = slice(k * PAD, (k + 1) * PAD)
-        numer = part_ref[:, rows, :].astype(jnp.float32)
-        numer = jnp.sum(share * numer, axis=0) + share_first * first_ref[rows, :].astype(jnp.float32)
-        denom = jnp.sum(share * total, axis=0) + share_first * total_first
-        merged.append((numer / denom).astype(jnp.bfloat16))
+        own = lane == 8 * row + 2 * k
+
+        def spread(x):
+            return jnp.sum(jnp.where(own, x, 0.0), axis=-1, keepdims=True)
+
+        rows = jnp.sum(spread(share[:, None, :]) * numer[k], axis=0)
+        rows = rows + spread(share_first) * numer_first[k]
+        merged.append(jnp.where(row < ROWS, rows, 0.0).astype(jnp.bfloat16))
     merged = jnp.concatenate(merged, axis=0)
     merged = jnp.dot(
         pad_matrix((QROWS, PROWS), 1), merged, preferred_element_type=jnp.float32
@@ -326,7 +335,7 @@
         first_kernel,
         in_specs=[*vmem(1), *hbm(1)],
         out_specs=vmem(1)[0],
-        out_shape=bf16(CHUNK, HEAD),
+        out_shape=bf16(PROWS, HEAD),
         scratch_shapes=scratch((), 8),
         compiler_params=pltpu.CompilerParams(vmem_limit_bytes=8 * 2**20),
     )(held, pool)
@@ -337,7 +346,7 @@
         attend_kernel,
         in_specs=[*vmem(1), *hbm(1), pl.BlockSpec(memory_space=pl.ANY)],
         out_specs=vmem(1)[0],
-        out_shape=bf16(PLACES, CHUNK, HEAD),
+        out_shape=bf16(PLACES, PROWS, HEAD),
         scratch_shapes=[
             *scratch((PLACES,), PLACES),
             pltpu.SMEM((PLACES + 1,), jnp.int32),

time: 57.1 us -> 55.5 us (0.972)
  waiting for transfers between devices: 19.9 us -> 17.7 us
  starting transfers between devices: 19.7 us -> 20.4 us
    all_to_all x1, waiting for transfers between devices: 4.95 us -> 2.74 us  [body(): lax.all_to_all(parts, 'pool', 0, 0, tiled=True, axis_index_groups=GROUPS)]
    ppermute x1, starting transfers between devices: 4.79 us -> 5.37 us  [body(): part_first = lax.ppermute(attend_first(first, pool), 'pool', PREVIOUS)]
where the time goes in v5:
time: 55.5 us; the launch traced here: 55.1 us
  starting transfers between devices  20.4 us (37%)
  waiting for transfers between devices  17.7 us (32%)
  Pallas kernels  16.3 us (29%)
  between operations  0.7 us (1%)
    ppermute x1, waiting for transfers between devices, body(): first = lax.ppermute(first, 'pool', NEXT)  12 us
    all_to_all x1, starting transfers between devices, body(): lax.all_to_all(sent, 'pool', 0, 0, tiled=True, axis_index_groups=GROUPS)  10.9 us
    pallas_call x1, Pallas kernels, attend_blocks(): pl.pallas_call(attend_kernel, in_specs=[*vmem(1), *hbm(1), pl.BlockSpec(m...  10.7 us
    ppermute x1, starting transfers between devices, body(): part_first = lax.ppermute(attend_first(first, pool), 'pool', PREVIOUS)  5.37 us
    all_to_all x1, starting transfers between devices, body(): lax.all_to_all(parts, 'pool', 0, 0, tiled=True, axis_index_groups=GROUPS)  4.11 us
    all_to_all x1, waiting for transfers between devices, body(): lax.all_to_all(parts, 'pool', 0, 0, tiled=True, axis_index_groups=GROUPS)  2.74 us
    pallas_call x1, Pallas kernels, attend_first(): pl.pallas_call(first_kernel, in_specs=[*vmem(1), *hbm(1)], out_specs=vmem...  2.59 us
    pallas_call x1, Pallas kernels, pack(): pl.pallas_call(pack_kernel, in_specs=[pl.BlockSpec(memory_space=pltpu.SME...  1.73 us
  transfers between devices with their start and end apart: 4, of which 4 were waited for; matrix products, arithmetic and copies ran while one was open for 0% of the time, Pallas kernels for 5%

profile of v5, /device:TPU:0, one launch (start us, length us, event | category | flops | bytes accessed | tf_op | source)
XLA Modules:
  0.0 55.1 jit_solution(3934497353490406097)
XLA Ops:
  0.7 1.7 %shard_map.46 = (bf16[32,64,128]{2,1,0:T(8,128)(2,1)}, bf16[64,128]{1,0:T(8,128)(2,1)S(1)}) custom-call(s32[1]{0:T(128)S(6)} %copy.6.length_ref, s32[32]{0:T(128)} %table_hbm.1, bf16[28,2,128]{2,1,0:T(2,128)(2,1)} %bitcast.13), custom_call_target="tpu_custom_call" | custom-call | tf_op jit(solution)/shard_map/pallas_call | solution.py:307
  2.4 10.9 %all-to-all-start = ((bf16[32,64,128]{2,1,0:T(8,128)(2,1)}), bf16[32,64,128]{2,1,0:T(8,128)(2,1)S(1)}, u32[]{:S(2)}, u32[]{:S(2)}) async-start(bf16[32,64,128]{2,1,0:T(8,128)(2,1)} %get-tuple-element.7), calls=%async_computation | async-start | bytes 1048576 | tf_op jit(solution)/shard_map/all_to_all | solution.py:382
  13.3 0.1 collective-permute-start
  13.4 12.0 %collective-permute-done._.held_ref = bf16[64,128]{1,0:T(8,128)(2,1)S(1)} collective-permute-done((bf16[64,128]{1,0:T(8,128)(2,1)S(1)}, bf16[64,128]{1,0:T(8,128)(2,1)S(1)}, u32[]{:S(2)}, u32[]{:S(2)}) %collective-permute-start) | collective-permute-done | bytes 16416 | tf_op jit(solution)/shard_map/ppermute | solution.py:381
  25.4 1.4 %all-to-all-done.held_ref = bf16[32,64,128]{2,1,0:T(8,128)(2,1)S(1)} async-done(((bf16[32,64,128]{2,1,0:T(8,128)(2,1)}), bf16[32,64,128]{2,1,0:T(8,128)(2,1)S(1)}, u32[]{:S(2)}, u32[]{:S(2)}) %all-to-all-start) | async-done | bytes 524320 | tf_op jit(solution)/shard_map/all_to_all | solution.py:382
  26.8 10.7 %shard_map.47 = bf16[32,64,128]{2,1,0:T(8,128)(2,1)} custom-call(bf16[32,64,128]{2,1,0:T(8,128)(2,1)S(1)} %all-to-all-done.held_ref, bf16[32,2048,128]{2,1,0:T(8,128)(2,1)} %bitcast.11, bf16[64,128]{1,0:T(8,128)(2,1)S(1)} %collective-permute-done._.held_ref), custom_call_target="tpu_custom_call" | custom-call | tf_op jit(solution)/shard_map/pallas_call | solution.py:345
  37.6 4.1 %all-to-all-start.1 = ((bf16[32,64,128]{2,1,0:T(8,128)(2,1)}), bf16[32,64,128]{2,1,0:T(8,128)(2,1)S(1)}, u32[]{:S(2)}, u32[]{:S(2)}) async-start(bf16[32,64,128]{2,1,0:T(8,128)(2,1)} %shard_map.47), calls=%async_computation.1 | async-start | bytes 1048576 | tf_op jit(solution)/shard_map/all_to_all | solution.py:385
  41.7 2.6 %shard_map.48 = bf16[64,128]{1,0:T(8,128)(2,1)S(1)} custom-call(bf16[64,128]{1,0:T(8,128)(2,1)S(1)} %collective-permute-done._.held_ref, bf16[32,2048,128]{2,1,0:T(8,128)(2,1)} %bitcast.12), custom_call_target="tpu_custom_call" | custom-call | tf_op jit(solution)/shard_map/pallas_call | solution.py:334
  44.3 5.4 %collective-permute-start.1 = (bf16[64,128]{1,0:T(8,128)(2,1)S(1)}, bf16[64,128]{1,0:T(8,128)(2,1)S(1)}, u32[]{:S(2)}, u32[]{:S(2)}) collective-permute-start(bf16[64,128]{1,0:T(8,128)(2,1)S(1)} %shard_map.48), channel_id=1, source_target_pairs={{1,0},{2,1},{3,2},{4,3},{5,4},{6,5},{7,6},{8,7},{9,8},{10,9},{11,1... | collective-permute-start | bytes 49160 | tf_op jit(solution)/shard_map/ppermute | solution.py:384
  49.7 1.4 %collective-permute-done.1.first_ref = bf16[64,128]{1,0:T(8,128)(2,1)S(1)} collective-permute-done((bf16[64,128]{1,0:T(8,128)(2,1)S(1)}, bf16[64,128]{1,0:T(8,128)(2,1)S(1)}, u32[]{:S(2)}, u32[]{:S(2)}) %collective-permute-start.1) | collective-permute-done | bytes 16416 | tf_op jit(solution)/shard_map/ppermute | solution.py:384
  51.1 2.7 %all-to-all-done.1.part_ref = bf16[32,64,128]{2,1,0:T(8,128)(2,1)S(1)} async-done(((bf16[32,64,128]{2,1,0:T(8,128)(2,1)}), bf16[32,64,128]{2,1,0:T(8,128)(2,1)S(1)}, u32[]{:S(2)}, u32[]{:S(2)}) %all-to-all-start.1) | async-done | bytes 524320 | tf_op jit(solution)/shard_map/all_to_all | solution.py:385
  53.9 1.2 %shard_map.49 = bf16[28,2,128]{2,1,0:T(2,128)(2,1)} custom-call(bf16[32,64,128]{2,1,0:T(8,128)(2,1)S(1)} %all-to-all-done.1.part_ref, bf16[64,128]{1,0:T(8,128)(2,1)S(1)} %collective-permute-done.1.first_ref), custom_call_target="tpu_custom_call" | custom-call | tf_op jit(solution)/shard_map/pallas_call | solution.py:360
Async XLA Ops:
  2.4 24.4 %all-to-all-start = ((bf16[32,64,128]{2,1,0:T(8,128)(2,1)}), bf16[32,64,128]{2,1,0:T(8,128)(2,1)S(1)}, u32[]{:S(2)}, u32[]{:S(2)}) async-start(bf16[32,64,128]{2,1,0:T(8,128)(2,1)} %get-tuple-element.7), calls=%async_computation | async-start | bytes 1048576 | tf_op jit(solution)/shard_map/all_to_all | solution.py:382
  13.3 12.1 %collective-permute-start = (bf16[64,128]{1,0:T(8,128)(2,1)S(1)}, bf16[64,128]{1,0:T(8,128)(2,1)S(1)}, u32[]{:S(2)}, u32[]{:S(2)}) collective-permute-start(bf16[64,128]{1,0:T(8,128)(2,1)S(1)} %get-tuple-element.8), channel_id=1, source_target_pairs={{0,1},{1,2},{2,3},{3,4},{4,5},{5,6},{6,7},{7,8},{8,9},{9,10},{10,1... | collective-permute-start | bytes 49160 | tf_op jit(solution)/shard_map/ppermute | solution.py:381
  37.6 16.3 %all-to-all-start.1 = ((bf16[32,64,128]{2,1,0:T(8,128)(2,1)}), bf16[32,64,128]{2,1,0:T(8,128)(2,1)S(1)}, u32[]{:S(2)}, u32[]{:S(2)}) async-start(bf16[32,64,128]{2,1,0:T(8,128)(2,1)} %shard_map.47), calls=%async_computation.1 | async-start | bytes 1048576 | tf_op jit(solution)/shard_map/all_to_all | solution.py:385
  44.3 6.8 %collective-permute-start.1 = (bf16[64,128]{1,0:T(8,128)(2,1)S(1)}, bf16[64,128]{1,0:T(8,128)(2,1)S(1)}, u32[]{:S(2)}, u32[]{:S(2)}) collective-permute-start(bf16[64,128]{1,0:T(8,128)(2,1)S(1)} %shard_map.48), channel_id=1, source_target_pairs={{1,0},{2,1},{3,2},{4,3},{5,4},{6,5},{7,6},{8,7},{9,8},{10,9},{11,1... | collective-permute-start | bytes 49160 | tf_op jit(solution)/shard_map/ppermute | solution.py:384

commit v6 on v5

--- a/solution.py
+++ b/solution.py
@@ -29,7 +29,7 @@
 
 
 def my_member():
-    return lax.axis_index("pool") // STRIDE
+    return lax.axis_index("pool") >> 2
 
 
 def iota(shape, dim):
@@ -69,17 +69,17 @@
     length = length_ref[0]
     row, lane = iota((PAD, HEAD), 0), iota((PAD, HEAD), 1)
     is_meta = row == META
-    length_lanes = jnp.where(lane == 1, length // 128, jnp.where(lane == 2, length % 128, 0))
+    length_lanes = jnp.where(lane == 1, length >> 7, jnp.where(lane == 2, length & 127, 0))
     head = padded[:PAD]
     rest = padded[PAD:].astype(jnp.bfloat16)
 
     def chunk_head(place):
-        slot = table_ref[place] % PLACES
+        slot = table_ref[place] & (PLACES - 1)
         meta = jnp.where(lane == 0, slot, length_lanes).astype(jnp.float32)
         return jnp.where(is_meta, meta, head).astype(jnp.bfloat16)
 
     for i in range(PLACES):
-        sent_ref[i, :PAD, :] = chunk_head(lax.rem(i + PLACES - member, PLACES))
+        sent_ref[i, :PAD, :] = chunk_head((i + PLACES - member) & (PLACES - 1))
         sent_ref[i, PAD:, :] = rest
     first_ref[:PAD, :] = chunk_head(0)
     first_ref[PAD:, :] = rest
@@ -189,11 +189,11 @@
     def load(slot):
         return pltpu.make_async_copy(pool_ref.at[slot], blocks.at[slot], load_sems.at[slot])
 
-    for slot in range(PLACES):
-        load(slot).start()
     member = my_member()
     meta_vmem[...] = meta_row(held_ref[:, :PAD, :])
     copy = start_scalars(meta_vmem, meta_smem, sem)
+    for slot in range(PLACES):
+        load(slot).start()
     empty = jnp.where(iota((PROWS, HEAD), 0) == ROWS, HIDDEN, 0.0).astype(jnp.bfloat16)
     for i in range(PLACES):
         part_ref[i] = empty
@@ -201,7 +201,7 @@
     copy.wait()
 
     def visible(i):
-        place = lax.rem(member + PLACES - i, PLACES)
+        place = (member + PLACES - i) & (PLACES - 1)
         return meta_smem[i, 1] * 128 + meta_smem[i, 2] + 1 - place * BLOCK
 
     for i in range(PLACES):
@@ -220,8 +220,9 @@
         weigh(blocks.at[slot], scores.at[slot], peaks.at[slot], part_ref.at[owner_at[slot]])
 
     for work, unroll in ((score_one, SCORE_UNROLL), (weigh_one, WEIGH_UNROLL)):
-        rest = count % unroll
-        whole = count // unroll + (rest > unroll // 2).astype(jnp.int32)
+        rest = count & (unroll - 1)
+        whole = lax.shift_right_logical(count, unroll.bit_length() - 1)
+        whole = whole + (rest > unroll // 2).astype(jnp.int32)
 
         def several(s, width, work=work, unroll=unroll):
             slots = [todo[jnp.minimum(s * unroll + u, count - 1)] for u in range(width)]
@@ -241,9 +242,14 @@
 
         lax.fori_loop(0, whole, step, 0)
 
-        @pl.when((rest > 0) & (rest <= unroll // 2))
-        def _(several=several, whole=whole, unroll=unroll):
-            several(whole, unroll // 2)
+        width = unroll // 2
+        while width:
+
+            @pl.when((rest > width // 2) & (rest <= width))
+            def _(several=several, whole=whole, width=width):
+                several(whole, width)
+
+            width //= 2
 
     for slot in range(PLACES):
 

time: 55.5 us -> 55.1 us (level)
  waiting for transfers between devices: 17.7 us -> 18.5 us
    ppermute x1, starting transfers between devices: 5.37 us -> 4.48 us  [body(): part_first = lax.ppermute(attend_first(first, pool), 'pool', PREVIOUS)]
    all_to_all x1, waiting for transfers between devices: 2.74 us -> 3.63 us  [body(): lax.all_to_all(parts, 'pool', 0, 0, tiled=True, axis_index_groups=GROUPS)]
where the time goes in v6:
time: 55.1 us; the launch traced here: 55 us
  starting transfers between devices  19.9 us (36%)
  waiting for transfers between devices  18.5 us (34%)
  Pallas kernels  15.9 us (29%)
  between operations  0.7 us (1%)
    ppermute x1, waiting for transfers between devices, body(): first = lax.ppermute(first, 'pool', NEXT)  12 us
    all_to_all x1, starting transfers between devices, body(): lax.all_to_all(sent, 'pool', 0, 0, tiled=True, axis_index_groups=GROUPS)  10.9 us
    pallas_call x1, Pallas kernels, attend_blocks(): pl.pallas_call(attend_kernel, in_specs=[*vmem(1), *hbm(1), pl.BlockSpec(m...  10.3 us
    ppermute x1, starting transfers between devices, body(): part_first = lax.ppermute(attend_first(first, pool), 'pool', PREVIOUS)  4.48 us
    all_to_all x1, starting transfers between devices, body(): lax.all_to_all(parts, 'pool', 0, 0, tiled=True, axis_index_groups=GROUPS)  4.45 us
    all_to_all x1, waiting for transfers between devices, body(): lax.all_to_all(parts, 'pool', 0, 0, tiled=True, axis_index_groups=GROUPS)  3.63 us
    pallas_call x1, Pallas kernels, attend_first(): pl.pallas_call(first_kernel, in_specs=[*vmem(1), *hbm(1)], out_specs=vmem...  2.59 us
    pallas_call x1, Pallas kernels, pack(): pl.pallas_call(pack_kernel, in_specs=[pl.BlockSpec(memory_space=pltpu.SME...  1.72 us
  transfers between devices with their start and end apart: 4, of which 4 were waited for; matrix products, arithmetic and copies ran while one was open for 0% of the time, Pallas kernels for 5%

profile of v6, /device:TPU:0, one launch (start us, length us, event | category | flops | bytes accessed | tf_op | source)
XLA Modules:
  0.0 55.0 jit_solution(18196161845221056498)
XLA Ops:
  0.7 1.7 %shard_map.46 = (bf16[32,64,128]{2,1,0:T(8,128)(2,1)}, bf16[64,128]{1,0:T(8,128)(2,1)S(1)}) custom-call(s32[1]{0:T(128)S(6)} %copy.6.length_ref, s32[32]{0:T(128)} %table_hbm.1, bf16[28,2,128]{2,1,0:T(2,128)(2,1)} %bitcast.13), custom_call_target="tpu_custom_call" | custom-call | tf_op jit(solution)/shard_map/pallas_call | solution.py:313
  2.4 10.9 %all-to-all-start = ((bf16[32,64,128]{2,1,0:T(8,128)(2,1)}), bf16[32,64,128]{2,1,0:T(8,128)(2,1)S(1)}, u32[]{:S(2)}, u32[]{:S(2)}) async-start(bf16[32,64,128]{2,1,0:T(8,128)(2,1)} %get-tuple-element.7), calls=%async_computation | async-start | bytes 1048576 | tf_op jit(solution)/shard_map/all_to_all | solution.py:388
  13.3 0.1 collective-permute-start
  13.4 12.0 %collective-permute-done._.held_ref = bf16[64,128]{1,0:T(8,128)(2,1)S(1)} collective-permute-done((bf16[64,128]{1,0:T(8,128)(2,1)S(1)}, bf16[64,128]{1,0:T(8,128)(2,1)S(1)}, u32[]{:S(2)}, u32[]{:S(2)}) %collective-permute-start) | collective-permute-done | bytes 16416 | tf_op jit(solution)/shard_map/ppermute | solution.py:387
  25.4 1.4 %all-to-all-done.held_ref = bf16[32,64,128]{2,1,0:T(8,128)(2,1)S(1)} async-done(((bf16[32,64,128]{2,1,0:T(8,128)(2,1)}), bf16[32,64,128]{2,1,0:T(8,128)(2,1)S(1)}, u32[]{:S(2)}, u32[]{:S(2)}) %all-to-all-start) | async-done | bytes 524320 | tf_op jit(solution)/shard_map/all_to_all | solution.py:388
  26.8 10.3 %shard_map.47 = bf16[32,64,128]{2,1,0:T(8,128)(2,1)} custom-call(bf16[32,64,128]{2,1,0:T(8,128)(2,1)S(1)} %all-to-all-done.held_ref, bf16[32,2048,128]{2,1,0:T(8,128)(2,1)} %bitcast.11, bf16[64,128]{1,0:T(8,128)(2,1)S(1)} %collective-permute-done._.held_ref), custom_call_target="tpu_custom_call" | custom-call | tf_op jit(solution)/shard_map/pallas_call | solution.py:351
  37.1 4.5 %all-to-all-start.1 = ((bf16[32,64,128]{2,1,0:T(8,128)(2,1)}), bf16[32,64,128]{2,1,0:T(8,128)(2,1)S(1)}, u32[]{:S(2)}, u32[]{:S(2)}) async-start(bf16[32,64,128]{2,1,0:T(8,128)(2,1)} %shard_map.47), calls=%async_computation.1 | async-start | bytes 1048576 | tf_op jit(solution)/shard_map/all_to_all | solution.py:391
  41.6 2.6 %shard_map.48 = bf16[64,128]{1,0:T(8,128)(2,1)S(1)} custom-call(bf16[64,128]{1,0:T(8,128)(2,1)S(1)} %collective-permute-done._.held_ref, bf16[32,2048,128]{2,1,0:T(8,128)(2,1)} %bitcast.12), custom_call_target="tpu_custom_call" | custom-call | tf_op jit(solution)/shard_map/pallas_call | solution.py:340
  44.2 4.5 %collective-permute-start.1 = (bf16[64,128]{1,0:T(8,128)(2,1)S(1)}, bf16[64,128]{1,0:T(8,128)(2,1)S(1)}, u32[]{:S(2)}, u32[]{:S(2)}) collective-permute-start(bf16[64,128]{1,0:T(8,128)(2,1)S(1)} %shard_map.48), channel_id=1, source_target_pairs={{1,0},{2,1},{3,2},{4,3},{5,4},{6,5},{7,6},{8,7},{9,8},{10,9},{11,1... | collective-permute-start | bytes 49160 | tf_op jit(solution)/shard_map/ppermute | solution.py:390
  48.7 1.4 %collective-permute-done.1.first_ref = bf16[64,128]{1,0:T(8,128)(2,1)S(1)} collective-permute-done((bf16[64,128]{1,0:T(8,128)(2,1)S(1)}, bf16[64,128]{1,0:T(8,128)(2,1)S(1)}, u32[]{:S(2)}, u32[]{:S(2)}) %collective-permute-start.1) | collective-permute-done | bytes 16416 | tf_op jit(solution)/shard_map/ppermute | solution.py:390
  50.1 3.6 %all-to-all-done.1.part_ref = bf16[32,64,128]{2,1,0:T(8,128)(2,1)S(1)} async-done(((bf16[32,64,128]{2,1,0:T(8,128)(2,1)}), bf16[32,64,128]{2,1,0:T(8,128)(2,1)S(1)}, u32[]{:S(2)}, u32[]{:S(2)}) %all-to-all-start.1) | async-done | bytes 524320 | tf_op jit(solution)/shard_map/all_to_all | solution.py:391
  53.8 1.2 %shard_map.49 = bf16[28,2,128]{2,1,0:T(2,128)(2,1)} custom-call(bf16[32,64,128]{2,1,0:T(8,128)(2,1)S(1)} %all-to-all-done.1.part_ref, bf16[64,128]{1,0:T(8,128)(2,1)S(1)} %collective-permute-done.1.first_ref), custom_call_target="tpu_custom_call" | custom-call | tf_op jit(solution)/shard_map/pallas_call | solution.py:366
Async XLA Ops:
  2.4 24.4 %all-to-all-start = ((bf16[32,64,128]{2,1,0:T(8,128)(2,1)}), bf16[32,64,128]{2,1,0:T(8,128)(2,1)S(1)}, u32[]{:S(2)}, u32[]{:S(2)}) async-start(bf16[32,64,128]{2,1,0:T(8,128)(2,1)} %get-tuple-element.7), calls=%async_computation | async-start | bytes 1048576 | tf_op jit(solution)/shard_map/all_to_all | solution.py:388
  13.3 12.1 %collective-permute-start = (bf16[64,128]{1,0:T(8,128)(2,1)S(1)}, bf16[64,128]{1,0:T(8,128)(2,1)S(1)}, u32[]{:S(2)}, u32[]{:S(2)}) collective-permute-start(bf16[64,128]{1,0:T(8,128)(2,1)S(1)} %get-tuple-element.8), channel_id=1, source_target_pairs={{0,1},{1,2},{2,3},{3,4},{4,5},{5,6},{6,7},{7,8},{8,9},{9,10},{10,1... | collective-permute-start | bytes 49160 | tf_op jit(solution)/shard_map/ppermute | solution.py:387
  37.1 16.6 %all-to-all-start.1 = ((bf16[32,64,128]{2,1,0:T(8,128)(2,1)}), bf16[32,64,128]{2,1,0:T(8,128)(2,1)S(1)}, u32[]{:S(2)}, u32[]{:S(2)}) async-start(bf16[32,64,128]{2,1,0:T(8,128)(2,1)} %shard_map.47), calls=%async_computation.1 | async-start | bytes 1048576 | tf_op jit(solution)/shard_map/all_to_all | solution.py:391
  44.2 5.9 %collective-permute-start.1 = (bf16[64,128]{1,0:T(8,128)(2,1)S(1)}, bf16[64,128]{1,0:T(8,128)(2,1)S(1)}, u32[]{:S(2)}, u32[]{:S(2)}) collective-permute-start(bf16[64,128]{1,0:T(8,128)(2,1)S(1)} %shard_map.48), channel_id=1, source_target_pairs={{1,0},{2,1},{3,2},{4,3},{5,4},{6,5},{7,6},{8,7},{9,8},{10,9},{11,1... | collective-permute-start | bytes 49160 | tf_op jit(solution)/shard_map/ppermute | solution.py:390

commit v7 on v6

--- a/solution.py
+++ b/solution.py
@@ -19,8 +19,7 @@
 LINES = BLOCK * KVH * 2
 TILE = 256
 META = ROWS
-SCORE_UNROLL = 4
-WEIGH_UNROLL = 8
+EARLY = 12
 LOG2_SCALE = 1.4426950408889634 / HEAD**0.5
 HIDDEN = -(2.0**120)
 GROUPS = [[STRIDE * i + r for i in range(PLACES)] for r in range(STRIDE)]
@@ -192,7 +191,7 @@
     member = my_member()
     meta_vmem[...] = meta_row(held_ref[:, :PAD, :])
     copy = start_scalars(meta_vmem, meta_smem, sem)
-    for slot in range(PLACES):
+    for slot in range(EARLY):
         load(slot).start()
     empty = jnp.where(iota((PROWS, HEAD), 0) == ROWS, HIDDEN, 0.0).astype(jnp.bfloat16)
     for i in range(PLACES):
@@ -209,8 +208,14 @@
         owner_at[slot] = jnp.where(visible(i) >= 0, i, -1)
     count = jnp.int32(0)
     for slot in range(PLACES):
+        seen = owner_at[slot] >= 0
         todo[count] = jnp.int32(slot)
-        count = count + (owner_at[slot] >= 0).astype(jnp.int32)
+        count = count + seen.astype(jnp.int32)
+        if slot >= EARLY:
+
+            @pl.when(seen)
+            def _(slot=slot):
+                load(slot).start()
 
     def score_one(slot):
         i = owner_at[slot]
@@ -219,39 +224,43 @@
     def weigh_one(slot):
         weigh(blocks.at[slot], scores.at[slot], peaks.at[slot], part_ref.at[owner_at[slot]])
 
-    for work, unroll in ((score_one, SCORE_UNROLL), (weigh_one, WEIGH_UNROLL)):
-        rest = count & (unroll - 1)
-        whole = lax.shift_right_logical(count, unroll.bit_length() - 1)
-        whole = whole + (rest > unroll // 2).astype(jnp.int32)
-
-        def several(s, width, work=work, unroll=unroll):
-            slots = [todo[jnp.minimum(s * unroll + u, count - 1)] for u in range(width)]
+    for work, narrow in ((score_one, 2), (weigh_one, 0)):
+
+        def several(start, width, work=work):
+            slots = [todo[jnp.minimum(start + u, count - 1)] for u in range(width)]
             if work is score_one:
                 for u in range(width):
 
-                    @pl.when(s * unroll + u < count)
+                    @pl.when(start + u < count)
                     def _(u=u):
                         load(slots[u]).wait()
 
             for slot in slots:
                 work(slot)
 
-        def step(s, carry, unroll=unroll, several=several):
-            several(s, unroll)
-            return carry
-
-        lax.fori_loop(0, whole, step, 0)
-
-        width = unroll // 2
-        while width:
+        def steps(start, width, number, several=several):
+            def step(s, carry):
+                several(start + s * width, width)
+                return carry
+
+            lax.fori_loop(0, number, step, 0)
+
+        start = jnp.int32(0)
+        if narrow:
+            number = jnp.minimum(count >> 2, narrow)
+            steps(start, 4, number)
+            start = 4 * number
+        rest = (count - start) & 7
+        number = ((count - start) >> 3) + (rest > 4).astype(jnp.int32)
+        steps(start, 8, number)
+        start = start + 8 * number
+        for width in (4, 2, 1):
 
             @pl.when((rest > width // 2) & (rest <= width))
-            def _(several=several, whole=whole, width=width):
-                several(whole, width)
-
-            width //= 2
-
-    for slot in range(PLACES):
+            def _(several=several, start=start, width=width):
+                several(start, width)
+
+    for slot in range(EARLY):
 
         @pl.when(owner_at[slot] < 0)
         def _(slot=slot):

time: 55.1 us -> 54.7 us (level)
  starting transfers between devices: 19.9 us -> 19.2 us
where the time goes in v7:
time: 54.7 us; the launch traced here: 54.5 us
  starting transfers between devices  19.2 us (35%)
  waiting for transfers between devices  18.8 us (34%)
  Pallas kernels  15.7 us (29%)
  between operations  0.7 us (1%)
    ppermute x1, waiting for transfers between devices, body(): first = lax.ppermute(first, 'pool', NEXT)  12 us
    all_to_all x1, starting transfers between devices, body(): lax.all_to_all(sent, 'pool', 0, 0, tiled=True, axis_index_groups=GROUPS)  10.9 us
    pallas_call x1, Pallas kernels, attend_blocks(): pl.pallas_call(attend_kernel, in_specs=[*vmem(1), *hbm(1), pl.BlockSpec(m...  10.2 us
    ppermute x1, starting transfers between devices, body(): part_first = lax.ppermute(attend_first(first, pool), 'pool', PREVIOUS)  4.38 us
    all_to_all x1, waiting for transfers between devices, body(): lax.all_to_all(parts, 'pool', 0, 0, tiled=True, axis_index_groups=GROUPS)  3.9 us
    all_to_all x1, starting transfers between devices, body(): lax.all_to_all(parts, 'pool', 0, 0, tiled=True, axis_index_groups=GROUPS)  3.9 us
    pallas_call x1, Pallas kernels, attend_first(): pl.pallas_call(first_kernel, in_specs=[*vmem(1), *hbm(1)], out_specs=vmem...  2.59 us
    pallas_call x1, Pallas kernels, pack(): pl.pallas_call(pack_kernel, in_specs=[pl.BlockSpec(memory_space=pltpu.SME...  1.72 us
  transfers between devices with their start and end apart: 4, of which 4 were waited for; matrix products, arithmetic and copies ran while one was open for 0% of the time, Pallas kernels for 5%

profile of v7, /device:TPU:0, one launch (start us, length us, event | category | flops | bytes accessed | tf_op | source)
XLA Modules:
  0.0 54.5 jit_solution(4790083671857692874)
XLA Ops:
  0.7 1.7 %shard_map.46 = (bf16[32,64,128]{2,1,0:T(8,128)(2,1)}, bf16[64,128]{1,0:T(8,128)(2,1)S(1)}) custom-call(s32[1]{0:T(128)S(6)} %copy.6.length_ref, s32[32]{0:T(128)} %table_hbm.1, bf16[28,2,128]{2,1,0:T(2,128)(2,1)} %bitcast.13), custom_call_target="tpu_custom_call" | custom-call | tf_op jit(solution)/shard_map/pallas_call | solution.py:322
  2.4 10.9 %all-to-all-start = ((bf16[32,64,128]{2,1,0:T(8,128)(2,1)}), bf16[32,64,128]{2,1,0:T(8,128)(2,1)S(1)}, u32[]{:S(2)}, u32[]{:S(2)}) async-start(bf16[32,64,128]{2,1,0:T(8,128)(2,1)} %get-tuple-element.7), calls=%async_computation | async-start | bytes 1048576 | tf_op jit(solution)/shard_map/all_to_all | solution.py:397
  13.3 0.1 collective-permute-start
  13.4 12.0 %collective-permute-done._.held_ref = bf16[64,128]{1,0:T(8,128)(2,1)S(1)} collective-permute-done((bf16[64,128]{1,0:T(8,128)(2,1)S(1)}, bf16[64,128]{1,0:T(8,128)(2,1)S(1)}, u32[]{:S(2)}, u32[]{:S(2)}) %collective-permute-start) | collective-permute-done | bytes 16416 | tf_op jit(solution)/shard_map/ppermute | solution.py:396
  25.4 1.4 %all-to-all-done.held_ref = bf16[32,64,128]{2,1,0:T(8,128)(2,1)S(1)} async-done(((bf16[32,64,128]{2,1,0:T(8,128)(2,1)}), bf16[32,64,128]{2,1,0:T(8,128)(2,1)S(1)}, u32[]{:S(2)}, u32[]{:S(2)}) %all-to-all-start) | async-done | bytes 524320 | tf_op jit(solution)/shard_map/all_to_all | solution.py:397
  26.8 10.2 %shard_map.47 = bf16[32,64,128]{2,1,0:T(8,128)(2,1)} custom-call(bf16[32,64,128]{2,1,0:T(8,128)(2,1)S(1)} %all-to-all-done.held_ref, bf16[32,2048,128]{2,1,0:T(8,128)(2,1)} %bitcast.11, bf16[64,128]{1,0:T(8,128)(2,1)S(1)} %collective-permute-done._.held_ref), custom_call_target="tpu_custom_call" | custom-call | tf_op jit(solution)/shard_map/pallas_call | solution.py:360
  37.0 3.9 %all-to-all-start.1 = ((bf16[32,64,128]{2,1,0:T(8,128)(2,1)}), bf16[32,64,128]{2,1,0:T(8,128)(2,1)S(1)}, u32[]{:S(2)}, u32[]{:S(2)}) async-start(bf16[32,64,128]{2,1,0:T(8,128)(2,1)} %shard_map.47), calls=%async_computation.1 | async-start | bytes 1048576 | tf_op jit(solution)/shard_map/all_to_all | solution.py:400
  40.9 2.6 %shard_map.48 = bf16[64,128]{1,0:T(8,128)(2,1)S(1)} custom-call(bf16[64,128]{1,0:T(8,128)(2,1)S(1)} %collective-permute-done._.held_ref, bf16[32,2048,128]{2,1,0:T(8,128)(2,1)} %bitcast.12), custom_call_target="tpu_custom_call" | custom-call | tf_op jit(solution)/shard_map/pallas_call | solution.py:349
  43.5 4.4 %collective-permute-start.1 = (bf16[64,128]{1,0:T(8,128)(2,1)S(1)}, bf16[64,128]{1,0:T(8,128)(2,1)S(1)}, u32[]{:S(2)}, u32[]{:S(2)}) collective-permute-start(bf16[64,128]{1,0:T(8,128)(2,1)S(1)} %shard_map.48), channel_id=1, source_target_pairs={{1,0},{2,1},{3,2},{4,3},{5,4},{6,5},{7,6},{8,7},{9,8},{10,9},{11,1... | collective-permute-start | bytes 49160 | tf_op jit(solution)/shard_map/ppermute | solution.py:399
  47.9 1.4 %collective-permute-done.1.first_ref = bf16[64,128]{1,0:T(8,128)(2,1)S(1)} collective-permute-done((bf16[64,128]{1,0:T(8,128)(2,1)S(1)}, bf16[64,128]{1,0:T(8,128)(2,1)S(1)}, u32[]{:S(2)}, u32[]{:S(2)}) %collective-permute-start.1) | collective-permute-done | bytes 16416 | tf_op jit(solution)/shard_map/ppermute | solution.py:399
  49.4 3.9 %all-to-all-done.1.part_ref = bf16[32,64,128]{2,1,0:T(8,128)(2,1)S(1)} async-done(((bf16[32,64,128]{2,1,0:T(8,128)(2,1)}), bf16[32,64,128]{2,1,0:T(8,128)(2,1)S(1)}, u32[]{:S(2)}, u32[]{:S(2)}) %all-to-all-start.1) | async-done | bytes 524320 | tf_op jit(solution)/shard_map/all_to_all | solution.py:400
  53.3 1.2 %shard_map.49 = bf16[28,2,128]{2,1,0:T(2,128)(2,1)} custom-call(bf16[32,64,128]{2,1,0:T(8,128)(2,1)S(1)} %all-to-all-done.1.part_ref, bf16[64,128]{1,0:T(8,128)(2,1)S(1)} %collective-permute-done.1.first_ref), custom_call_target="tpu_custom_call" | custom-call | tf_op jit(solution)/shard_map/pallas_call | solution.py:375
Async XLA Ops:
  2.4 24.4 %all-to-all-start = ((bf16[32,64,128]{2,1,0:T(8,128)(2,1)}), bf16[32,64,128]{2,1,0:T(8,128)(2,1)S(1)}, u32[]{:S(2)}, u32[]{:S(2)}) async-start(bf16[32,64,128]{2,1,0:T(8,128)(2,1)} %get-tuple-element.7), calls=%async_computation | async-start | bytes 1048576 | tf_op jit(solution)/shard_map/all_to_all | solution.py:397
  13.3 12.1 %collective-permute-start = (bf16[64,128]{1,0:T(8,128)(2,1)S(1)}, bf16[64,128]{1,0:T(8,128)(2,1)S(1)}, u32[]{:S(2)}, u32[]{:S(2)}) collective-permute-start(bf16[64,128]{1,0:T(8,128)(2,1)S(1)} %get-tuple-element.8), channel_id=1, source_target_pairs={{0,1},{1,2},{2,3},{3,4},{4,5},{5,6},{6,7},{7,8},{8,9},{9,10},{10,1... | collective-permute-start | bytes 49160 | tf_op jit(solution)/shard_map/ppermute | solution.py:396
  37.0 16.2 %all-to-all-start.1 = ((bf16[32,64,128]{2,1,0:T(8,128)(2,1)}), bf16[32,64,128]{2,1,0:T(8,128)(2,1)S(1)}, u32[]{:S(2)}, u32[]{:S(2)}) async-start(bf16[32,64,128]{2,1,0:T(8,128)(2,1)} %shard_map.47), calls=%async_computation.1 | async-start | bytes 1048576 | tf_op jit(solution)/shard_map/all_to_all | solution.py:400
  43.5 5.8 %collective-permute-start.1 = (bf16[64,128]{1,0:T(8,128)(2,1)S(1)}, bf16[64,128]{1,0:T(8,128)(2,1)S(1)}, u32[]{:S(2)}, u32[]{:S(2)}) collective-permute-start(bf16[64,128]{1,0:T(8,128)(2,1)S(1)} %shard_map.48), channel_id=1, source_target_pairs={{1,0},{2,1},{3,2},{4,3},{5,4},{6,5},{7,6},{8,7},{9,8},{10,9},{11,1... | collective-permute-start | bytes 49160 | tf_op jit(solution)/shard_map/ppermute | solution.py:399

commit v8 on v7

--- a/solution.py
+++ b/solution.py
@@ -19,7 +19,7 @@
 LINES = BLOCK * KVH * 2
 TILE = 256
 META = ROWS
-EARLY = 12
+EARLY = 8
 LOG2_SCALE = 1.4426950408889634 / HEAD**0.5
 HIDDEN = -(2.0**120)
 GROUPS = [[STRIDE * i + r for i in range(PLACES)] for r in range(STRIDE)]

time: 54.7 us -> 54.6 us (level)
  starting transfers between devices: 19.2 us -> 20.9 us
  waiting for transfers between devices: 18.8 us -> 17.6 us
  Pallas kernels: 15.7 us -> 14.9 us
    all_to_all x1, waiting for transfers between devices: 3.9 us -> 2.68 us  [body(): lax.all_to_all(parts, 'pool', 0, 0, tiled=True, axis_index_groups=GROUPS)]
    ppermute x1, starting transfers between devices: 4.38 us -> 5.44 us  [body(): part_first = lax.ppermute(attend_first(first, pool), 'pool', PREVIOUS)]
    pallas_call x1, Pallas kernels: 10.2 us -> 9.33 us  [attend_blocks(): pl.pallas_call(attend_kernel, in_specs=[*vmem(1), *hbm(1), pl.BlockSpec(m...]
    all_to_all x1, starting transfers between devices: 3.9 us -> 4.51 us  [body(): lax.all_to_all(parts, 'pool', 0, 0, tiled=True, axis_index_groups=GROUPS)]
where the time goes in v8:
time: 54.6 us; the launch traced here: 54.1 us
  starting transfers between devices  20.9 us (38%)
  waiting for transfers between devices  17.6 us (32%)
  Pallas kernels  14.9 us (27%)
  between operations  0.7 us (1%)
    ppermute x1, waiting for transfers between devices, body(): first = lax.ppermute(first, 'pool', NEXT)  12 us
    all_to_all x1, starting transfers between devices, body(): lax.all_to_all(sent, 'pool', 0, 0, tiled=True, axis_index_groups=GROUPS)  10.9 us
    pallas_call x1, Pallas kernels, attend_blocks(): pl.pallas_call(attend_kernel, in_specs=[*vmem(1), *hbm(1), pl.BlockSpec(m...  9.33 us
    ppermute x1, starting transfers between devices, body(): part_first = lax.ppermute(attend_first(first, pool), 'pool', PREVIOUS)  5.44 us
    all_to_all x1, starting transfers between devices, body(): lax.all_to_all(parts, 'pool', 0, 0, tiled=True, axis_index_groups=GROUPS)  4.51 us
    all_to_all x1, waiting for transfers between devices, body(): lax.all_to_all(parts, 'pool', 0, 0, tiled=True, axis_index_groups=GROUPS)  2.68 us
    pallas_call x1, Pallas kernels, attend_first(): pl.pallas_call(first_kernel, in_specs=[*vmem(1), *hbm(1)], out_specs=vmem...  2.59 us
    pallas_call x1, Pallas kernels, pack(): pl.pallas_call(pack_kernel, in_specs=[pl.BlockSpec(memory_space=pltpu.SME...  1.72 us
  transfers between devices with their start and end apart: 4, of which 4 were waited for; matrix products, arithmetic and copies ran while one was open for 0% of the time, Pallas kernels for 5%

profile of v8, /device:TPU:0, one launch (start us, length us, event | category | flops | bytes accessed | tf_op | source)
XLA Modules:
  0.0 54.1 jit_solution(9722762181798168182)
XLA Ops:
  0.7 1.7 %shard_map.46 = (bf16[32,64,128]{2,1,0:T(8,128)(2,1)}, bf16[64,128]{1,0:T(8,128)(2,1)S(1)}) custom-call(s32[1]{0:T(128)S(6)} %copy.6.length_ref, s32[32]{0:T(128)} %table_hbm.1, bf16[28,2,128]{2,1,0:T(2,128)(2,1)} %bitcast.13), custom_call_target="tpu_custom_call" | custom-call | tf_op jit(solution)/shard_map/pallas_call | solution.py:322
  2.4 10.9 %all-to-all-start = ((bf16[32,64,128]{2,1,0:T(8,128)(2,1)}), bf16[32,64,128]{2,1,0:T(8,128)(2,1)S(1)}, u32[]{:S(2)}, u32[]{:S(2)}) async-start(bf16[32,64,128]{2,1,0:T(8,128)(2,1)} %get-tuple-element.7), calls=%async_computation | async-start | bytes 1048576 | tf_op jit(solution)/shard_map/all_to_all | solution.py:397
  13.3 0.1 collective-permute-start
  13.4 12.0 %collective-permute-done._.held_ref = bf16[64,128]{1,0:T(8,128)(2,1)S(1)} collective-permute-done((bf16[64,128]{1,0:T(8,128)(2,1)S(1)}, bf16[64,128]{1,0:T(8,128)(2,1)S(1)}, u32[]{:S(2)}, u32[]{:S(2)}) %collective-permute-start) | collective-permute-done | bytes 16416 | tf_op jit(solution)/shard_map/ppermute | solution.py:396
  25.4 1.4 %all-to-all-done.held_ref = bf16[32,64,128]{2,1,0:T(8,128)(2,1)S(1)} async-done(((bf16[32,64,128]{2,1,0:T(8,128)(2,1)}), bf16[32,64,128]{2,1,0:T(8,128)(2,1)S(1)}, u32[]{:S(2)}, u32[]{:S(2)}) %all-to-all-start) | async-done | bytes 524320 | tf_op jit(solution)/shard_map/all_to_all | solution.py:397
  26.8 9.3 %shard_map.47 = bf16[32,64,128]{2,1,0:T(8,128)(2,1)} custom-call(bf16[32,64,128]{2,1,0:T(8,128)(2,1)S(1)} %all-to-all-done.held_ref, bf16[32,2048,128]{2,1,0:T(8,128)(2,1)} %bitcast.11, bf16[64,128]{1,0:T(8,128)(2,1)S(1)} %collective-permute-done._.held_ref), custom_call_target="tpu_custom_call" | custom-call | tf_op jit(solution)/shard_map/pallas_call | solution.py:360
  36.2 4.5 %all-to-all-start.1 = ((bf16[32,64,128]{2,1,0:T(8,128)(2,1)}), bf16[32,64,128]{2,1,0:T(8,128)(2,1)S(1)}, u32[]{:S(2)}, u32[]{:S(2)}) async-start(bf16[32,64,128]{2,1,0:T(8,128)(2,1)} %shard_map.47), calls=%async_computation.1 | async-start | bytes 1048576 | tf_op jit(solution)/shard_map/all_to_all | solution.py:400
  40.7 2.6 %shard_map.48 = bf16[64,128]{1,0:T(8,128)(2,1)S(1)} custom-call(bf16[64,128]{1,0:T(8,128)(2,1)S(1)} %collective-permute-done._.held_ref, bf16[32,2048,128]{2,1,0:T(8,128)(2,1)} %bitcast.12), custom_call_target="tpu_custom_call" | custom-call | tf_op jit(solution)/shard_map/pallas_call | solution.py:349
  43.3 5.4 %collective-permute-start.1 = (bf16[64,128]{1,0:T(8,128)(2,1)S(1)}, bf16[64,128]{1,0:T(8,128)(2,1)S(1)}, u32[]{:S(2)}, u32[]{:S(2)}) collective-permute-start(bf16[64,128]{1,0:T(8,128)(2,1)S(1)} %shard_map.48), channel_id=1, source_target_pairs={{1,0},{2,1},{3,2},{4,3},{5,4},{6,5},{7,6},{8,7},{9,8},{10,9},{11,1... | collective-permute-start | bytes 49160 | tf_op jit(solution)/shard_map/ppermute | solution.py:399
  48.7 1.4 %collective-permute-done.1.first_ref = bf16[64,128]{1,0:T(8,128)(2,1)S(1)} collective-permute-done((bf16[64,128]{1,0:T(8,128)(2,1)S(1)}, bf16[64,128]{1,0:T(8,128)(2,1)S(1)}, u32[]{:S(2)}, u32[]{:S(2)}) %collective-permute-start.1) | collective-permute-done | bytes 16416 | tf_op jit(solution)/shard_map/ppermute | solution.py:399
  50.2 2.7 %all-to-all-done.1.part_ref = bf16[32,64,128]{2,1,0:T(8,128)(2,1)S(1)} async-done(((bf16[32,64,128]{2,1,0:T(8,128)(2,1)}), bf16[32,64,128]{2,1,0:T(8,128)(2,1)S(1)}, u32[]{:S(2)}, u32[]{:S(2)}) %all-to-all-start.1) | async-done | bytes 524320 | tf_op jit(solution)/shard_map/all_to_all | solution.py:400
  52.8 1.2 %shard_map.49 = bf16[28,2,128]{2,1,0:T(2,128)(2,1)} custom-call(bf16[32,64,128]{2,1,0:T(8,128)(2,1)S(1)} %all-to-all-done.1.part_ref, bf16[64,128]{1,0:T(8,128)(2,1)S(1)} %collective-permute-done.1.first_ref), custom_call_target="tpu_custom_call" | custom-call | tf_op jit(solution)/shard_map/pallas_call | solution.py:375
Async XLA Ops:
  2.4 24.4 %all-to-all-start = ((bf16[32,64,128]{2,1,0:T(8,128)(2,1)}), bf16[32,64,128]{2,1,0:T(8,128)(2,1)S(1)}, u32[]{:S(2)}, u32[]{:S(2)}) async-start(bf16[32,64,128]{2,1,0:T(8,128)(2,1)} %get-tuple-element.7), calls=%async_computation | async-start | bytes 1048576 | tf_op jit(solution)/shard_map/all_to_all | solution.py:397
  13.3 12.1 %collective-permute-start = (bf16[64,128]{1,0:T(8,128)(2,1)S(1)}, bf16[64,128]{1,0:T(8,128)(2,1)S(1)}, u32[]{:S(2)}, u32[]{:S(2)}) collective-permute-start(bf16[64,128]{1,0:T(8,128)(2,1)S(1)} %get-tuple-element.8), channel_id=1, source_target_pairs={{0,1},{1,2},{2,3},{3,4},{4,5},{5,6},{6,7},{7,8},{8,9},{9,10},{10,1... | collective-permute-start | bytes 49160 | tf_op jit(solution)/shard_map/ppermute | solution.py:396
  36.2 16.7 %all-to-all-start.1 = ((bf16[32,64,128]{2,1,0:T(8,128)(2,1)}), bf16[32,64,128]{2,1,0:T(8,128)(2,1)S(1)}, u32[]{:S(2)}, u32[]{:S(2)}) async-start(bf16[32,64,128]{2,1,0:T(8,128)(2,1)} %shard_map.47), calls=%async_computation.1 | async-start | bytes 1048576 | tf_op jit(solution)/shard_map/all_to_all | solution.py:400
  43.3 6.9 %collective-permute-start.1 = (bf16[64,128]{1,0:T(8,128)(2,1)S(1)}, bf16[64,128]{1,0:T(8,128)(2,1)S(1)}, u32[]{:S(2)}, u32[]{:S(2)}) collective-permute-start(bf16[64,128]{1,0:T(8,128)(2,1)S(1)} %shard_map.48), channel_id=1, source_target_pairs={{1,0},{2,1},{3,2},{4,3},{5,4},{6,5},{7,6},{8,7},{9,8},{10,9},{11,1... | collective-permute-start | bytes 49160 | tf_op jit(solution)/shard_map/ppermute | solution.py:399
